TPU v7x, 128 devices: a whole 4x4x4 slice. The times are simulated.
128 devices in a mesh: blk: 16 (over z, x_hi, core), dp: 8 (over y, x_lo).
Axes of the slice: x: 4 (x_hi: 2, x_lo: 2; x = x_hi * 2 + x_lo), y: 4, z: 4, core: 2. Of those that a mesh axis runs over, the one named last changes fastest.
Arguments:
- tokens: bfloat16 [65536, 2048], P(('blk', 'dp')), may hold values from -24 to 24
- segment_ids: int32 [128, 512], P(('blk', 'dp')), may hold values from -1 to 31, as said below
- owners: int32 [128, 32], P(('blk', 'dp')), may hold values from -1 to 127, as said below
- images: bfloat16 [2048, 1152], P(('blk', 'dp')), may hold values from -6 to 6
- weight: bfloat16 [2048, 2048], replicated, may hold values from -0.125 to 0.125
- gain: float32 [2048], replicated, may hold values from 0.25 to 1.75
- head: bfloat16 [2048, 1152], replicated, may hold values from -0.125 to 0.125
- logit_params: float32 [2], replicated, as said below
Outputs:
- loss: float32 [2048], P(('blk', 'dp'))
- d_tokens: bfloat16 [65536, 2048], P(('blk', 'dp'))
- d_weight: float32 [2048, 2048], P(('blk', 'dp'))
- d_gain: float32 [2048], replicated
- d_images: float32 [2048, 1152], P(('blk', 'dp'))
Inputs may be any that keep to these rules, and one draw needn't show every extreme that they name: `owners`: entry c of device row r is -1 for an empty caption slot, else the slot, among the 128 images of the devices with the same blk index, of the image that caption describes; over those devices every slot is named exactly once. The captions of one device name at most 4 slots of any one device (slot // 16), and in every group some device names exactly 4 of every device's slots. `segment_ids`: A caption slot holds tokens exactly when its owners entry is not -1; those tokens are one run of 1 to 32 positions, the runs in slot order from position 0, and -1 after the last run. `logit_params`: entry 0 is the log temperature, entry 1 the bias.
All inputs are finite; a program needn't handle non-finite values.
Results may differ from a plain program's by a relative error of at most 0.019.
Values may be sent and summed in bfloat16 or wider, within the bound.
A program may use at most 128 MiB of HBM per device.

v0:
```python
import jax
import jax.numpy as jnp
from jax import lax
from jax.sharding import PartitionSpec as P


def project_rows(rows_in, head):
    proj = jnp.dot(rows_in, head, preferred_element_type=jnp.float32)
    scale_inv = lax.rsqrt(jnp.sum(proj * proj, axis=1, keepdims=True) + 1e-06)
    return (proj * scale_inv, scale_inv)


def unit_backward(unit, scale_inv, grad):
    return scale_inv * (grad - unit * jnp.sum(unit * grad, axis=1, keepdims=True))


def pair_terms(left, right, left_ids, right_ids, scale, bias):
    logits = (
        scale
        * lax.dot_general(left, right, (((1,), (1,)), ((), ())), preferred_element_type=jnp.float32)
        + bias
    )
    sign = jnp.where(left_ids[:, None] == right_ids[None, :], 1.0, -1.0)
    loss_part = jnp.sum(jax.nn.softplus(-sign * logits), axis=1)
    coef = (-scale * sign * jax.nn.sigmoid(-sign * logits)).astype(jnp.bfloat16)
    return (loss_part, coef)


def per_device(tokens, segment_ids, owners, images, weight, gain, head, logit_params):
    f32 = jnp.float32
    bf16 = jnp.bfloat16
    rows, width = tokens.shape
    caps = owners.shape[1]
    batch, embed_width = images.shape
    groups = lax.axis_size("dp")
    capp = caps // groups
    total = batch * groups * lax.axis_size("blk")
    seg = segment_ids[0]
    owned = owners[0]
    x = tokens.astype(f32)
    inv_rms = lax.rsqrt(jnp.mean(x * x, axis=1, keepdims=True) + 1e-06)
    normed = (x * inv_rms * gain).astype(bf16)
    hidden = (x + jnp.dot(normed, weight, preferred_element_type=f32)).astype(bf16)
    select = (seg[None, :] == jnp.arange(caps, dtype=jnp.int32)[:, None]).astype(bf16)
    counts = jnp.maximum(jnp.sum(select.astype(f32), axis=1), 1.0)[:, None]
    pooled = (jnp.dot(select, hidden, preferred_element_type=f32) / counts).astype(bf16)
    live = owned >= 0
    dest = jnp.where(live, owned // batch, -1)
    place = jnp.where(live, owned % batch + 1, 0)
    match = (dest[:, None] == jnp.arange(groups, dtype=jnp.int32)[None, :]).astype(jnp.int32)
    rank = jnp.sum((jnp.cumsum(match, axis=0) - 1) * match, axis=1)
    slot = jnp.where(live, dest * capp + rank, -1)
    route = (slot[None, :] == jnp.arange(groups * capp, dtype=jnp.int32)[:, None]).astype(bf16)
    send_place = jnp.sum(route.astype(f32) * place.astype(f32)[None, :], axis=1).astype(bf16)
    sent_rows = jnp.dot(route, pooled, preferred_element_type=f32).astype(bf16)
    moved_rows, moved_place = (
        lax.all_to_all(
            sent_rows.reshape(groups, capp, width), "dp", split_axis=0, concat_axis=0, tiled=True
        ),
        lax.all_to_all(
            send_place.reshape(groups, capp), "dp", split_axis=0, concat_axis=0, tiled=True
        ),
    )
    arrival = (
        moved_place.reshape(-1).astype(f32)[None, :] == (jnp.arange(batch) + 1).astype(f32)[:, None]
    ).astype(bf16)
    texts_pooled = jnp.dot(
        arrival, moved_rows.reshape(-1, width), preferred_element_type=f32
    ).astype(bf16)
    text_unit, scale_inv = project_rows(texts_pooled, head)
    text_embed = text_unit.astype(bf16)
    img = images.astype(f32)
    img_inv = lax.rsqrt(jnp.sum(img * img, axis=1, keepdims=True) + 1e-06)
    img_unit = img * img_inv
    img_embed = img_unit.astype(bf16)
    scale = jnp.exp(logit_params[0])
    bias = logit_params[1]
    device_flat = lax.axis_index("blk") * groups + lax.axis_index("dp")
    my_ids = device_flat * batch + jnp.arange(batch, dtype=jnp.int32)
    group_text = lax.all_gather(text_embed, "dp", axis=0, tiled=True)
    piece = lax.all_gather(group_text, "blk", axis=0, tiled=True)
    piece_ids = jnp.arange(piece.shape[0], dtype=jnp.int32)
    loss_part, coef = pair_terms(img_embed, piece, my_ids, piece_ids, scale, bias)
    dimg = jnp.dot(coef, piece, preferred_element_type=f32)
    folded = (loss_part, dimg, coef)
    loss_acc = folded[0]
    dimg = folded[1]
    coef_all = folded[2]
    dtext = lax.psum_scatter(
        lax.dot_general(coef_all, img_embed, (((0,), (0,)), ((), ())), preferred_element_type=f32),
        ("blk", "dp"),
        scatter_dimension=0,
        tiled=True,
    )
    d_images = img_inv * (dimg - img_unit * jnp.sum(img_unit * dimg, axis=1, keepdims=True))
    dproj = unit_backward(text_unit, scale_inv, dtext).astype(bf16)
    dpooled_owner = lax.dot_general(
        dproj, head, (((1,), (1,)), ((), ())), preferred_element_type=f32
    ).astype(bf16)
    back_rows = lax.dot_general(
        arrival, dpooled_owner, (((0,), (0,)), ((), ())), preferred_element_type=f32
    ).astype(bf16)
    returned = lax.all_to_all(
        back_rows.reshape(groups, capp, width), "dp", split_axis=0, concat_axis=0, tiled=True
    )
    dpooled = lax.dot_general(
        route, returned.reshape(-1, width), (((0,), (0,)), ((), ())), preferred_element_type=f32
    )
    dcap = (dpooled / counts).astype(bf16)
    dhidden = lax.dot_general(
        select, dcap, (((0,), (0,)), ((), ())), preferred_element_type=f32
    ).astype(bf16)
    dnorm = lax.dot_general(dhidden, weight, (((1,), (1,)), ((), ())), preferred_element_type=f32)
    d_weight = lax.psum_scatter(
        lax.dot_general(normed, dhidden, (((0,), (0,)), ((), ())), preferred_element_type=f32),
        ("blk", "dp"),
        scatter_dimension=0,
        tiled=True,
    )
    scaled = gain * dnorm
    dx = inv_rms * scaled - x * inv_rms * inv_rms * inv_rms * jnp.mean(
        x * scaled, axis=1, keepdims=True
    )
    d_tokens = (dhidden.astype(f32) + dx).astype(bf16)
    gain_part = jnp.sum(x * inv_rms * dnorm, axis=0)
    d_gain = lax.psum(gain_part, ("blk", "dp"))
    return (loss_acc / total, d_tokens, d_weight, d_gain, d_images)


def solution(mesh):
    in_specs = (
        P(("blk", "dp"), None),
        P(("blk", "dp"), None),
        P(("blk", "dp"), None),
        P(("blk", "dp"), None),
        P(),
        P(),
        P(),
        P(),
    )
    out_specs = (
        P(("blk", "dp")),
        P(("blk", "dp"), None),
        P(("blk", "dp"), None),
        P(),
        P(("blk", "dp"), None),
    )
    return jax.shard_map(
        per_device, mesh=mesh, in_specs=in_specs, out_specs=out_specs, check_vma=False
    )
```

profile of v0, /device:TPU:1, one launch (start us, length us, event | category | flops | bytes accessed | tf_op | source)
XLA Modules:
  0.0 1477.8 jit_solution(13530425932561282190)
XLA Ops:
  7.2 0.7 compare_select_fusion.1
  7.8 0.1 fusion.44
  7.9 0.1 reduce_window_sum.11
  8.0 0.2 select_reduce_fusion
  8.1 0.7 convert_bitcast_fusion
  8.8 0.1 multiply_reduce_fusion.2
  8.9 0.7 convert_element_type.131
  9.6 5.9 all-to-all-start
  15.6 0.8 convert_reduce_fusion
  16.4 2.1 fusion.10
  18.5 9.5 fusion.13
  28.0 0.0 copy-start.5
  28.0 0.0 copy-start.2
  28.0 0.2 convolution_convert_fusion.2
  28.2 0.7 reshape.120
  28.9 5.2 all-to-all-start.1
  34.0 0.0 all-gather.2.cloned.1.call-start
  34.1 0.1 reshape.124
  34.2 5.4 all-to-all-done.1
  39.6 3.3 multiply_reduce_fusion.1
  43.0 0.1 multiply_convert_fusion.1
  43.0 25.1 %all_gather.6 = bf16[128,1152]{1,0:T(8,128)(2,1)} all-gather(bf16[16,1152]{1,0:T(8,128)(2,1)S(1)} %multiply_convert_fusion.1), channel_id=1, replica_groups=mesh['blk'=16,'dp'=8] {'dp'}, dimensions={0}, use_global_device_ids=true | all-gather | bytes 331776 | tf_op jit(solution)/shard_map/all_gather | solution.py:80
  68.2 0.0 all-gather.2.cloned.1.call-update
  68.2 0.0 reduce-scatter.3.cloned.1.call-start
  68.2 0.6 fusion.67
  69.6 0.1 fusion.35
  69.7 64.2 %all-gather.2.cloned.1.call-done = bf16[2048,1152]{1,0:T(8,128)(2,1)} async-done(((bf16[128,1152]{1,0:T(8,128)(2,1)}), bf16[2048,1152]{1,0:T(8,128)(2,1)}) %all-gather.2.cloned.1.call-update) | async-done | bytes 4718608 | tf_op jit(solution)/shard_map/all_gather | solution.py:81
  133.8 4.4 fusion.27
  138.3 5.1 fusion.45
  143.4 0.0 reduce-scatter.3.cloned.1.call-update
  143.5 0.0 copy-start.3
  143.5 0.0 copy-start
  143.5 0.0 reduce-scatter.5.cloned.1.call-start
  143.5 635.5 %reduce-scatter.3.cloned.1.call-done = f32[16,1152]{1,0:T(8,128)} async-done(((f32[2048,1152]{1,0:T(8,128)}), f32[16,1152]{1,0:T(8,128)}) %reduce-scatter.3.cloned.1.call-update) | async-done | bytes 73744 | tf_op jit(solution)/shard_map/reduce_scatter | solution.py:89
  779.0 1.1 multiply_reduce_fusion
  780.1 3.8 convolution_convert_fusion.1
  783.9 0.1 reshape.122
  784.0 8.2 all_to_all.16
  792.3 2.2 convolution_convert_fusion
  794.5 9.8 fusion.17
  804.2 0.0 reduce-scatter.5.cloned.1.call-update
  804.3 0.5 broadcast_multiply_fusion.1
  804.8 3.3 fusion.32
  808.1 0.7 fusion.34
  808.8 10.2 fusion.9
  819.0 80.1 %psum.7 = f32[2048]{0:T(1024)} all-reduce(f32[2048]{0:T(1024)S(1)} %get-tuple-element.5), channel_id=1, replica_groups=mesh['blk'=16,'dp'=8] {'blk','dp'}, use_global_device_ids=true, to_apply=%region_13.14 | all-reduce | flops 2048 | bytes 16384 | tf_op jit(solution)/shard_map/psum | solution.py:126
  899.1 5.9 fusion.8
  905.0 566.3 %reduce-scatter.5.cloned.1.call-done = f32[16,2048]{1,0:T(8,128)} async-done(((f32[2048,2048]{1,0:T(8,128)}), f32[16,2048]{1,0:T(8,128)}) %reduce-scatter.5.cloned.1.call-update) | async-done | bytes 131088 | tf_op jit(solution)/shard_map/reduce_scatter | solution.py:114
  (19 shorter events, 0.1 us)
Async XLA Ops:
  9.6 19.2 %all-to-all-start = ((bf16[8,1,4]{2,1,0:T(2,128)(2,1)}), bf16[8,1,4]{2,1,0:T(2,128)(2,1)S(1)}, u32[]{:S(2)}, u32[]{:S(2)}) async-start(bf16[8,1,4]{2,1,0:T(2,128)(2,1)} %convert_element_type.131), calls=%async_computation | async-start | bytes 8192 | tf_op jit(solution)/shard_map/all_to_all | solution.py:60
  28.0 40.3 %copy-start.5 = (f32[2]{0:T(128)S(1)}, f32[2]{0:T(128)}, u32[]{:S(2)}) copy-start(f32[2]{0:T(128)} %param.15) | copy-start | bytes 28
  28.0 41.6 %copy-start.2 = (bf16[16,1152]{1,0:T(8,128)(2,1)S(1)}, bf16[16,1152]{1,0:T(8,128)(2,1)}, u32[]{:S(2)}) copy-start(bf16[16,1152]{1,0:T(8,128)(2,1)} %param.11) | copy-start | bytes 110596
  28.9 10.7 all-to-all-start.1
  34.0 99.8 %all-gather.2.cloned.1.call-start = ((), (), s32[]{:S(2)}) async-start(), calls=%async_computation.5 | async-start | bytes 5013504 | tf_op jit(solution)/shard_map/all_gather | solution.py:81
  68.2 710.8 %reduce-scatter.3.cloned.1.call-start = ((), (), s32[]{:S(2)}) async-start(), calls=%async_computation.6 | async-start | bytes 9510912 | tf_op jit(solution)/shard_map/reduce_scatter | solution.py:89
  143.5 648.8 %copy-start.3 = (s32[1,512]{1,0:T(1,128)S(1)}, s32[1,512]{1,0:T(1,128)}, u32[]{:S(2)}) copy-start(s32[1,512]{1,0:T(1,128)} %param.9) | copy-start | bytes 6148
  143.5 651.0 %copy-start = (bf16[512,2048]{1,0:T(8,128)(2,1)S(1)}, bf16[512,2048]{1,0:T(8,128)(2,1)}, u32[]{:S(2)}) copy-start(bf16[512,2048]{1,0:T(8,128)(2,1)} %param.8) | copy-start | bytes 6291460
  143.5 651.0 %copy-start.4 = (f32[2048]{0:T(1024)S(1)}, f32[2048]{0:T(1024)}, u32[]{:S(2)}) copy-start(f32[2048]{0:T(1024)} %param.13) | copy-start | bytes 24580
  143.5 1327.8 %reduce-scatter.5.cloned.1.call-start = ((), (), s32[]{:S(2)}) async-start(), calls=%async_computation.7 | async-start | bytes 16908288 | tf_op jit(solution)/shard_map/reduce_scatter | solution.py:114
  804.3 4.6 copy-start.1
Sparse Core Ops, SparseCore 0:
  68.3 65.5 all-gather.1
  143.6 635.3 reduce-scatter.2
  804.4 666.8 reduce-scatter.4
where the time goes:
time: 1490 us; the launch traced here: 1480 us
  waiting for transfers between devices  1270 us (85%)
  blocking collectives  113 us (8%)
  matrix products  51.9 us (3%)
    reduce_scatter x1, waiting for transfers between devices, per_device(): lax.psum_scatter(lax.dot_general(coef_all, img_embed, (((0,), (0,)), ((),...  635 us
    reduce_scatter x1, waiting for transfers between devices, per_device(): lax.psum_scatter(lax.dot_general(normed, dhidden, (((0,), (0,)), ((), ())...  566 us
    psum x1, blocking collectives, per_device(): d_gain = lax.psum(gain_part, ('blk', 'dp'))  80.1 us
    all_gather x1, waiting for transfers between devices, per_device(): piece = lax.all_gather(group_text, 'blk', axis=0, tiled=True)  64.2 us
  transfers between devices with their start and end apart: 5, of which 4 were waited for; matrix products, arithmetic and copies ran while one was open for 2% of the time, Pallas kernels for 0%

commit v1 on v0

v1 whole, which is shorter than its diff:
```python
import functools

import jax
import jax.numpy as jnp
from jax import lax
from jax.experimental import pallas as pl
from jax.experimental.pallas import tpu as pltpu
from jax.sharding import PartitionSpec as P

f32 = jnp.float32
bf16 = jnp.bfloat16
MESH = pl.DeviceIdType.MESH

DT = 2048
E = 1152
ROWS = 512
CAPS = 32
NB = 16
ND = 8
TOTAL = 2048
PW = E + 128
PARTS = 3
PC = E // PARTS
ORDERS = (("x", "y", "z"), ("y", "z", "x"), ("z", "x", "y"))
TN = 512


def mm(a, b):
    return lax.dot_general(a, b, (((1,), (0,)), ((), ())), preferred_element_type=f32)


def mm_nt(a, b):
    return lax.dot_general(a, b, (((1,), (1,)), ((), ())), preferred_element_type=f32)


def split2(v):
    hi = v.astype(bf16)
    return hi, (v - hi.astype(f32)).astype(bf16)


def iota(shape, dim):
    return lax.broadcasted_iota(jnp.int32, shape, dim)


def kernel(
    tok_hbm, w_hbm, head_hbm, seg_ref, own_ref, img_ref, gain_ref, lp_ref,
    loss_out, dtok_hbm, dw_out, dgain_out, dimg_out,
    tok, wv, headv, img, lcol, segt, invc, xs, xp, npst, pooled, asrc, arcv, tbuf, dcap, stack,
    stage, bacc, rsacc, c3s, c3r, lbuf, gsrc, gbuf, g2,
    ld_sem, w_sem, st_sem,
    i_send, i_recv, ic_send, ic_recv, t_send, t_recv, tc_send, tc_recv, a_send, a_recv,
    c_send, c_recv, l_send, l_recv, g_send, g_recv, h_send, h_recv,
):
    b = lax.axis_index("blk")
    d = lax.axis_index("dp")
    z, xh, core = b // 4, (b // 2) % 2, b % 2
    y, xl = d // 2, d % 2
    x = xh * 2 + xl
    sib = (b + 1 - 2 * core, d)

    loads = []
    for i in range(4):
        cp = pltpu.make_async_copy(
            tok_hbm.at[pl.ds(i * 128, 128), :], tok.at[pl.ds(i * 128, 128), :], ld_sem.at[i]
        )
        cp.start()
        loads.append(cp)
    wloads = []
    for i in range(DT // TN):
        cp = pltpu.make_async_copy(
            w_hbm.at[:, pl.ds(i * TN, TN)], wv.at[:, pl.ds(i * TN, TN)], w_sem.at[i]
        )
        cp.start()
        wloads.append(cp)
    hload = pltpu.make_async_copy(head_hbm, headv, ld_sem.at[4])
    hload.start()

    barrier = pltpu.get_barrier_semaphore()
    for k in range(1, ND):
        pl.semaphore_signal(barrier, inc=1, device_id=(b, (d + k) % ND), device_id_type=MESH)
    for k in range(1, NB):
        pl.semaphore_signal(barrier, inc=1, device_id=((b + k) % NB, d), device_id_type=MESH)
    pl.semaphore_signal(
        barrier, inc=1, device_id=(z * 4 + (1 - xh) * 2 + core, y * 2 + 1 - xl), device_id_type=MESH
    )

    im = img_ref[...].astype(f32)
    img_inv = lax.rsqrt(jnp.sum(im * im, axis=1, keepdims=True) + 1e-06)
    img_unit = im * img_inv
    img[z, xh, core, y, xl] = img_unit.astype(bf16)

    pl.semaphore_wait(barrier, NB + ND - 1)

    sends = []

    def region(p, at):
        def pick(name):
            return slice(None) if at[name] is None else at[name]

        xx = at["x"]
        return img.at[
            pick("z"),
            slice(None) if xx is None else xx // 2,
            at["core"],
            pick("y"),
            slice(None) if xx is None else xx % 2,
            :,
            pl.ds(p * PC, PC),
        ]

    here = {"x": x, "y": y, "z": z, "core": core}

    def device(at):
        return (at["z"] * 4 + (at["x"] // 2) * 2 + at["core"], at["y"] * 2 + at["x"] % 2)

    def ring_copy(p, s, k, done, where, to):
        at = dict(where)
        for name in done:
            at[name] = None
        ref = region(p, at)
        return pltpu.make_async_remote_copy(
            src_ref=ref, dst_ref=ref, send_sem=i_send.at[p, s, k], recv_sem=i_recv.at[p, s, k],
            device_id=device(to), device_id_type=MESH,
        )

    def ring_send(p, s):
        order = ORDERS[p]
        axis, done = order[s], order[:s]
        for k in range(3):
            to = dict(here)
            to[axis] = (here[axis] + k + 1) % 4
            cp = ring_copy(p, s, k, done, here, to)
            cp.start()
            sends.append(cp)

    def ring_wait(p, s, k):
        order = ORDERS[p]
        axis, done = order[s], order[:s]
        frm = dict(here)
        frm[axis] = (here[axis] + 3 - k) % 4
        ring_copy(p, s, k, done, frm, frm).wait_recv()

    def core_copy(p, q, own):
        order = ORDERS[p]
        at = dict(here)
        for name in order[:2]:
            at[name] = None
        if q:
            at[order[2]] = (here[order[2]] + 4 - q) % 4
        if not own:
            at["core"] = 1 - core
        ref = region(p, at)
        return pltpu.make_async_remote_copy(
            src_ref=ref, dst_ref=ref, send_sem=ic_send.at[p, q], recv_sem=ic_recv.at[p, q],
            device_id=sib, device_id_type=MESH,
        )

    def core_send(p, q):
        cp = core_copy(p, q, True)
        cp.start()
        sends.append(cp)

    for p in range(PARTS):
        ring_send(p, 0)

    segf = seg_ref[...].astype(f32)
    segt[...] = jnp.broadcast_to(segf, (128, ROWS)).T
    lane = iota((128, 128), 1)
    cap_of = (lane % CAPS).astype(f32)
    kind = lane // CAPS

    def token_rows(i):
        loads[i].wait()
        rows = pl.ds(i * 128, 128)
        xx = tok[rows, :].astype(f32)
        inv = lax.rsqrt(jnp.sum(xx * xx, axis=1, keepdims=True) * (1.0 / DT) + 1e-06)
        invc[rows, :] = inv
        hi = inv.astype(bf16).astype(f32)
        lo = inv - hi
        val = jnp.where(kind == 0, 1.0, jnp.where(kind == 2, lo, hi))
        lcol[rows, :] = jnp.where(segt[rows, :] == cap_of, val, 0.0)

    token_rows(0)
    token_rows(1)
    for p in range(PARTS):
        for k in range(3):
            ring_wait(p, 0, k)
        ring_send(p, 1)
    token_rows(2)
    token_rows(3)

    lrow = lcol[...].T.astype(bf16)
    gain = gain_ref[...]

    def pool_tile(i, _):
        cols = pl.ds(pl.multiple_of(i * TN, TN), TN)
        acc = mm(lrow, tok[:, cols])
        xs[:, cols] = acc[0:CAPS]
        xpt = acc[CAPS : 2 * CAPS] + acc[2 * CAPS : 3 * CAPS]
        xp[:, cols] = xpt
        hi, lo = split2(xpt * gain_ref[:, cols])
        npst[0:CAPS, cols] = hi
        npst[CAPS : 2 * CAPS, cols] = lo
        return 0

    lax.fori_loop(0, DT // TN, pool_tile, 0)

    for p in range(PARTS):
        for k in range(3):
            ring_wait(p, 1, k)
        ring_send(p, 2)
        core_send(p, 0)

    sel = (jnp.broadcast_to(segf, (CAPS, ROWS)) == iota((CAPS, ROWS), 0).astype(f32)).astype(f32)
    rcount = 1.0 / jnp.maximum(jnp.sum(sel, axis=1, keepdims=True), 1.0)
    ownf = own_ref[...].astype(f32)
    own_col = jnp.sum(
        jnp.where(iota((CAPS, CAPS), 0) == iota((CAPS, CAPS), 1), jnp.broadcast_to(ownf, (CAPS, CAPS)), 0.0),
        axis=1,
        keepdims=True,
    )

    for i in range(DT // TN):
        wloads[i].wait()
        cols = pl.ds(i * TN, TN)
        yy = mm(npst[...], wv[:, cols])
        pooled[:, cols] = ((xs[:, cols] + yy[0:CAPS] + yy[CAPS : 2 * CAPS]) * rcount).astype(bf16)

    hload.wait()
    proj = mm(pooled[...], headv[...])
    scale_inv = lax.rsqrt(jnp.sum(proj * proj, axis=1, keepdims=True) + 1e-06)
    text_unit = proj * scale_inv
    text = text_unit.astype(bf16)
    tbuf[b, :, 0:E] = text
    tbuf[b, :, E:PW] = jnp.broadcast_to(own_col, (CAPS, 128)).astype(bf16)
    factor = scale_inv * rcount
    for j in range(NB):
        cols = pl.ds(j * 128, 128)
        asrc[j] = (xp[:, cols] * gain_ref[:, cols] * factor).astype(bf16)
    arcv[b] = asrc[b]

    def text_peer(k, sign):
        dz, dx = (k + 1) // 2, (k + 1) % 2
        return ((z + 4 + sign * dz) % 4) * 4 + ((xh + dx) % 2) * 2 + core

    def text_copy(k, idx, to):
        return pltpu.make_async_remote_copy(
            src_ref=tbuf.at[idx], dst_ref=tbuf.at[idx], send_sem=t_send.at[k], recv_sem=t_recv.at[k],
            device_id=(to, d), device_id_type=MESH,
        )

    def text_core(k, idx):
        return pltpu.make_async_remote_copy(
            src_ref=tbuf.at[idx], dst_ref=tbuf.at[idx], send_sem=tc_send.at[k], recv_sem=tc_recv.at[k],
            device_id=sib, device_id_type=MESH,
        )

    for k in range(7):
        cp = text_copy(k, b, text_peer(k, 1))
        cp.start()
        sends.append(cp)
    cp = text_core(7, b)
    cp.start()
    sends.append(cp)
    for k in range(NB - 1):
        to = (b + k + 1) % NB
        cp = pltpu.make_async_remote_copy(
            src_ref=asrc.at[to], dst_ref=arcv.at[b], send_sem=a_send.at[k], recv_sem=a_recv.at[k],
            device_id=(to, d), device_id_type=MESH,
        )
        cp.start()
        sends.append(cp)

    for p in range(PARTS):
        for k in range(3):
            ring_wait(p, 2, k)
            core_send(p, k + 1)
    for k in range(7):
        frm = text_peer(k, -1)
        text_copy(k, frm, frm).wait_recv()
        cp = text_core(k, frm)
        cp.start()
        sends.append(cp)
    for p in range(PARTS):
        for q in range(4):
            core_copy(p, q, False).wait_recv()

    scale = jnp.exp(jnp.full((1, 128), lp_ref[0], f32))[:, 0:1]
    bias = jnp.full((1, 128), lp_ref[1], f32)[:, 0:1]

    def pair(dots, gid, first):
        ids = (iota((1, dots.shape[1]), 1) + first).astype(f32)
        sgn = jnp.where(gid == ids, 1.0, -1.0)
        arg = -sgn * (scale * dots + bias)
        coef = (-scale * sgn) / (1.0 + jnp.exp(-arg))
        return arg, coef.astype(bf16)

    gid_own = jnp.where(own_col >= 0.0, own_col + (b * 128).astype(f32), -1.0)
    dtext = jnp.zeros((CAPS, E), f32)
    for c in range(4):
        chunk = img[c].reshape(512, E)
        _, coef = pair(mm_nt(text, chunk), gid_own, c * 512)
        dtext = dtext + mm(coef, chunk)
    dproj = (
        scale_inv * (dtext - text_unit * jnp.sum(text_unit * dtext, axis=1, keepdims=True))
    ).astype(bf16)
    live = jnp.where(own_col >= 0.0, rcount, 0.0)

    def dcap_tile(i, _):
        rows = pl.ds(pl.multiple_of(i * TN, TN), TN)
        dpool = mm_nt(dproj, headv[rows, :]).astype(bf16).astype(f32)
        dc = (dpool * live).astype(bf16)
        dcap[:, rows] = dc
        stack[0:CAPS, rows] = dc
        return 0

    lax.fori_loop(0, DT // TN, dcap_tile, 0)

    def dnorm_tile(i, _):
        rows = pl.ds(pl.multiple_of(i * TN, TN), TN)
        dn = mm_nt(dcap[...], wv[rows, :])
        gsrc[:, rows] = jnp.sum(xp[:, rows] * dn, axis=0, keepdims=True)
        hi, lo = split2(dn * gain_ref[:, rows])
        stack[CAPS : 2 * CAPS, rows] = hi
        stack[2 * CAPS : 3 * CAPS, rows] = hi
        stack[3 * CAPS : 4 * CAPS, rows] = lo
        return 0

    lax.fori_loop(0, DT // TN, dnorm_tile, 0)

    for r in range(16):
        gbuf[d, r : r + 1, :] = gsrc[:, r * 128 : (r + 1) * 128]

    def dp_copy(buf, src, idx, k, ssem, rsem):
        return pltpu.make_async_remote_copy(
            src_ref=src, dst_ref=buf.at[idx], send_sem=ssem.at[k], recv_sem=rsem.at[k],
            device_id=(b, (d + k + 1) % ND), device_id_type=MESH,
        )

    for k in range(ND - 1):
        cp = dp_copy(gbuf, gbuf.at[d], d, k, g_send, g_recv)
        cp.start()
        sends.append(cp)

    for k in range(7):
        frm = text_peer(k, -1)
        text_core(k, frm + 1 - 2 * core).wait_recv()
    text_core(7, sib[0]).wait_recv()
    for k in range(NB - 1):
        frm = (b + NB - 1 - k) % NB
        pltpu.make_async_remote_copy(
            src_ref=arcv.at[frm], dst_ref=arcv.at[frm], send_sem=a_send.at[k], recv_sem=a_recv.at[k],
            device_id=(frm, d), device_id_type=MESH,
        ).wait_recv()

    slots = NB * CAPS
    owner = tbuf[:, :, E:PW].reshape(slots, 128).astype(f32)[:, 0:1]
    block = (iota((slots, 1), 0) // CAPS * 128).astype(f32)
    gid = jnp.where(owner >= 0.0, owner + block, -1.0)
    share = arcv[...].reshape(slots, 128).astype(f32)
    share_t = share.T.astype(bf16)
    bacc[...] = jnp.zeros((128, E), f32)
    rsacc[...] = jnp.zeros((slots, 1), f32)

    def pair_chunk(c, _):
        chunk = img[c].reshape(512, E)
        dots = mm_nt(tbuf[:, :, 0:E].reshape(slots, E), chunk)
        _, coef = pair(dots, gid, c * 512)
        rsacc[...] += jnp.sum(coef.astype(f32) * dots, axis=1, keepdims=True)
        zt = mm(share_t, coef).astype(bf16)
        bacc[...] += mm(zt, chunk)
        return 0

    lax.fori_loop(0, 4, pair_chunk, 0)

    texts = tbuf[:, :, 0:E].reshape(slots, E)
    minus_t = (share * rsacc[...]).T.astype(bf16)
    bpart = bacc[...] - mm(minus_t, texts)
    group = img[z, xh, core].reshape(128, E)
    arg, coef = pair(mm_nt(texts, group), gid, b * 128)
    soft = jnp.maximum(arg, 0.0) + jnp.log1p(jnp.exp(-jnp.abs(arg)))
    lrow_part = jnp.sum(jnp.where(gid >= 0.0, soft, 0.0), axis=0, keepdims=True)
    dimg_part = mm(coef.astype(f32).T.astype(bf16), texts)
    c3s[:, :, 0:E] = dimg_part.reshape(ND, 16, E).astype(bf16)
    c3s[:, :, E : 2 * E] = bpart.reshape(ND, 16, E).astype(bf16)
    c3r[d] = c3s[d]
    lbuf[d] = jnp.broadcast_to(lrow_part, (8, 128))
    for k in range(ND - 1):
        cp = dp_copy(c3r, c3s.at[(d + k + 1) % ND], d, k, c_send, c_recv)
        cp.start()
        sends.append(cp)
        cp = dp_copy(lbuf, lbuf.at[d], d, k, l_send, l_recv)
        cp.start()
        sends.append(cp)

    for k in range(ND - 1):
        frm = (d + ND - 1 - k) % ND
        dp_copy(gbuf, gbuf.at[frm], frm, k, g_send, g_recv).wait_recv()
    g2[b] = jnp.sum(gbuf[...], axis=0)
    for k in range(NB - 1):
        cp = pltpu.make_async_remote_copy(
            src_ref=g2.at[b], dst_ref=g2.at[b], send_sem=h_send.at[k], recv_sem=h_recv.at[k],
            device_id=((b + k + 1) % NB, d), device_id_type=MESH,
        )
        cp.start()
        sends.append(cp)

    stores = []
    for i in range(4):
        rows = pl.ds(i * 128, 128)
        xb = tok[rows, :]
        lc = lcol[rows, :]
        q = mm_nt(xb, stack[...])
        mine = (segt[rows, :] == cap_of) & ((kind == 1) | (kind == 3))
        mean = jnp.sum(jnp.where(mine, q, 0.0), axis=1, keepdims=True) * (1.0 / DT)
        inv = invc[rows, :]
        drop = inv * inv * inv * mean
        full = mm(lc.astype(bf16), stack[...])
        stage[rows, :] = (full - xb.astype(f32) * drop).astype(bf16)
        cp = pltpu.make_async_copy(stage.at[rows, :], dtok_hbm.at[rows, :], st_sem.at[i])
        cp.start()
        stores.append(cp)

    for k in range(ND - 1):
        frm = (d + ND - 1 - k) % ND
        dp_copy(c3r, c3r.at[frm], frm, k, c_send, c_recv).wait_recv()
        dp_copy(lbuf, lbuf.at[frm], frm, k, l_send, l_recv).wait_recv()
    dimg = jnp.sum(c3r[:, :, 0:E].astype(f32), axis=0)
    bmine = jnp.sum(c3r[:, :, E : 2 * E].astype(f32), axis=0)
    dimg_out[...] = img_inv * (dimg - img_unit * jnp.sum(img_unit * dimg, axis=1, keepdims=True))
    hi, lo = split2(bmine)
    both = jnp.concatenate([hi, lo], axis=0)

    def dw_tile(i, _):
        rows = pl.ds(pl.multiple_of(i * TN, TN), TN)
        dw = mm_nt(both, headv[rows, :])
        dw_out[:, rows] = dw[0:16] + dw[16:32]
        return 0

    lax.fori_loop(0, DT // TN, dw_tile, 0)

    lsum = jnp.sum(lbuf[...], axis=0)[0:1] * (1.0 / TOTAL)
    col = jnp.sum(
        jnp.where(iota((16, 128), 1) == iota((16, 128), 0) + 16 * d, jnp.broadcast_to(lsum, (16, 128)), 0.0),
        axis=1,
        keepdims=True,
    )
    loss_out[...] = jnp.sum(jnp.where(iota((16, 16), 0) == iota((16, 16), 1), col, 0.0), axis=0, keepdims=True)

    for k in range(NB - 1):
        frm = (b + NB - 1 - k) % NB
        pltpu.make_async_remote_copy(
            src_ref=g2.at[frm], dst_ref=g2.at[frm], send_sem=h_send.at[k], recv_sem=h_recv.at[k],
            device_id=(frm, d), device_id_type=MESH,
        ).wait_recv()
    dgain_out[...] = jnp.sum(g2[...], axis=0)

    for cp in stores:
        cp.wait()
    for cp in sends:
        cp.wait_send()


def per_device(tokens, segment_ids, owners, images, weight, gain, head, logit_params):
    vmem = pl.BlockSpec(memory_space=pltpu.VMEM)
    hbm = pl.BlockSpec(memory_space=pl.ANY)
    dma = pltpu.SemaphoreType.DMA
    loss, d_tokens, d_weight, d_gain, d_images = pl.pallas_call(
        kernel,
        out_shape=(
            jax.ShapeDtypeStruct((1, 16), f32),
            jax.ShapeDtypeStruct((ROWS, DT), bf16),
            jax.ShapeDtypeStruct((16, DT), f32),
            jax.ShapeDtypeStruct((16, 128), f32),
            jax.ShapeDtypeStruct((16, E), f32),
        ),
        in_specs=[hbm, hbm, hbm, vmem, vmem, vmem, vmem, pl.BlockSpec(memory_space=pltpu.SMEM)],
        out_specs=(vmem, hbm, vmem, vmem, vmem),
        scratch_shapes=[
            pltpu.VMEM((ROWS, DT), bf16),
            pltpu.VMEM((DT, DT), bf16),
            pltpu.VMEM((DT, E), bf16),
            pltpu.VMEM((4, 2, 2, 4, 2, 16, E), bf16),
            pltpu.VMEM((ROWS, 128), f32),
            pltpu.VMEM((ROWS, 128), f32),
            pltpu.VMEM((ROWS, 1), f32),
            pltpu.VMEM((CAPS, DT), f32),
            pltpu.VMEM((CAPS, DT), f32),
            pltpu.VMEM((2 * CAPS, DT), bf16),
            pltpu.VMEM((CAPS, DT), bf16),
            pltpu.VMEM((NB, CAPS, 128), bf16),
            pltpu.VMEM((NB, CAPS, 128), bf16),
            pltpu.VMEM((NB, CAPS, PW), bf16),
            pltpu.VMEM((CAPS, DT), bf16),
            pltpu.VMEM((4 * CAPS, DT), bf16),
            pltpu.VMEM((ROWS, DT), bf16),
            pltpu.VMEM((128, E), f32),
            pltpu.VMEM((NB * CAPS, 1), f32),
            pltpu.VMEM((ND, 16, 2 * E), bf16),
            pltpu.VMEM((ND, 16, 2 * E), bf16),
            pltpu.VMEM((ND, 8, 128), f32),
            pltpu.VMEM((1, DT), f32),
            pltpu.VMEM((ND, 16, 128), f32),
            pltpu.VMEM((NB, 16, 128), f32),
            dma((5,)),
            dma((DT // TN,)),
            dma((4,)),
            dma((PARTS, 3, 3)),
            dma((PARTS, 3, 3)),
            dma((PARTS, 4)),
            dma((PARTS, 4)),
            dma((7,)),
            dma((7,)),
            dma((8,)),
            dma((8,)),
            dma((NB - 1,)),
            dma((NB - 1,)),
            dma((ND - 1,)),
            dma((ND - 1,)),
            dma((ND - 1,)),
            dma((ND - 1,)),
            dma((ND - 1,)),
            dma((ND - 1,)),
            dma((NB - 1,)),
            dma((NB - 1,)),
        ],
        compiler_params=pltpu.CompilerParams(
            collective_id=0, has_side_effects=True, vmem_limit_bytes=56 * 1024 * 1024
        ),
    )(tokens, weight, head, segment_ids, owners, images, gain.reshape(1, DT), logit_params)
    return loss.reshape(16), d_tokens, d_weight, d_gain.reshape(DT), d_images


def solution(mesh):
    rows = P(("blk", "dp"), None)
    return jax.shard_map(
        per_device,
        mesh=mesh,
        in_specs=(rows, rows, rows, rows, P(), P(), P(), P()),
        out_specs=(P(("blk", "dp")), rows, rows, P(), rows),
        check_vma=False,
    )
```

time: 1490 us -> 72.3 us (0.05)
  waiting for transfers between devices: 1270 us -> 0 us
  blocking collectives: 113 us -> 0 us
  Pallas kernels: 0 us -> 65.2 us
  matrix products: 51.9 us -> 0 us
    reduce_scatter x2 -> x0, waiting for transfers between devices: 1200 us -> none  [the longest x1 635 us: per_device(): lax.psum_scatter(lax.dot_general(coef_all, img_embed, (((0,), (0,)), ((),...]
    psum x1 -> x0, blocking collectives: 80.1 us -> none  [per_device(): d_gain = lax.psum(gain_part, ('blk', 'dp'))]
    pallas_call x0 -> x1, Pallas kernels: none -> 65.2 us  [per_device(): pl.pallas_call(kernel, out_shape=(jax.ShapeDtypeStruct((1, 16), f32), jax...]
    all_gather x1 -> x0, waiting for transfers between devices: 64.2 us -> none  [per_device(): piece = lax.all_gather(group_text, 'blk', axis=0, tiled=True)]
    dot_general x10 -> x0, matrix products: 51.9 us -> none  [the longest x1 10.2 us: per_device(): lax.dot_general(dhidden, weight, (((1,), (1,)), ((), ())), preferred_elem...]
    all_gather x1 -> x0, blocking collectives: 25.1 us -> none  [per_device(): group_text = lax.all_gather(text_embed, 'dp', axis=0, tiled=True)]
  transfers between devices with their start and end apart: 5 -> 0, of which waited for: 4 -> 0; matrix products, arithmetic and copies ran while one was open for 2% -> 0% of each run, Pallas kernels for 0% -> 0%
where the time goes in v1:
time: 72.3 us; the launch traced here: 72.1 us
  Pallas kernels  65.2 us (90%)
  local copies, waits for them, and re-layouts  6.28 us (9%)
    pallas_call x1, Pallas kernels, per_device(): pl.pallas_call(kernel, out_shape=(jax.ShapeDtypeStruct((1, 16), f32), jax...  65.2 us
    unnamed x11, local copies, waits for them, and re-layouts  6.28 us

profile of v1, /device:TPU:1, one launch (start us, length us, event | category | flops | bytes accessed | tf_op | source)
XLA Modules:
  0.0 72.1 jit_solution(2201022182096948590)
XLA Ops:
  0.6 65.2 %shard_map.119 = (f32[1,16]{1,0:T(1,128)}, bf16[512,2048]{1,0:T(8,128)(2,1)}, f32[16,2048]{1,0:T(8,128)}, f32[16,128]{1,0:T(8,128)}, f32[16,1152]{1,0:T(8,128)}) custom-call(bf16[512,2048]{1,0:T(8,128)(2,1)} %tok_hbm.1, bf16[2048,2048]{1,0:T(8,128)(2,1)} %w_hbm.1, bf16[2048,1152]{1,0:T(8,128)(2,1)} %head_hbm.1, s32[1,512]{1,0:T(1,128)} %seg_ref.1, ...), custom_call_target="tpu_custom_call" | custom-call | tf_op jit(solution)/shard_map/pallas_call | solution.py:468
  65.8 1.2 %copy.18 = f32[16]{0:T(128)} copy(f32[16]{0:T(128)} %bitcast.5) | data formatting | bytes 128
  67.0 0.0 copy-start
  67.0 0.0 copy-start.2
  67.0 0.0 copy-start.1
  67.0 3.2 %copy.19 = bf16[512,2048]{1,0:T(8,128)(2,1)} copy(bf16[512,2048]{1,0:T(8,128)(2,1)} %get-tuple-element.21) | data formatting | bytes 4194304
  70.2 0.0 copy-done
  70.2 0.7 copy.20
  70.9 0.0 copy-done.2
  70.9 0.6 copy.21
  71.5 0.0 copy-done.1
  71.5 0.6 copy.22
Async XLA Ops:
  67.0 3.2 %copy-start = (f32[16,2048]{1,0:T(8,128)S(1)}, f32[16,2048]{1,0:T(8,128)}, u32[]{:S(2)}) copy-start(f32[16,2048]{1,0:T(8,128)} %get-tuple-element.22) | copy-start | bytes 393220
  67.0 3.9 %copy-start.2 = (f32[16,128]{1,0:T(8,128)S(1)}, f32[16,128]{1,0:T(8,128)}, u32[]{:S(2)}) copy-start(f32[16,128]{1,0:T(8,128)} %get-tuple-element.13) | copy-start | bytes 24580
  67.0 4.5 %copy-start.1 = (f32[16,1152]{1,0:T(8,128)S(1)}, f32[16,1152]{1,0:T(8,128)}, u32[]{:S(2)}) copy-start(f32[16,1152]{1,0:T(8,128)} %get-tuple-element.24) | copy-start | bytes 221188

commit v2 on v1

v2 whole, which is shorter than its diff:
```python
import functools

import jax
import jax.numpy as jnp
from jax import lax
from jax.experimental import pallas as pl
from jax.experimental.pallas import tpu as pltpu
from jax.sharding import PartitionSpec as P

f32 = jnp.float32
bf16 = jnp.bfloat16
MESH = pl.DeviceIdType.MESH

DT = 2048
E = 1152
ROWS = 512
CAPS = 32
NB = 16
ND = 8
TOTAL = 2048
PW = E + 128
PARTS = 3
ORDERS = (("x", "y", "z"), ("y", "z", "x"), ("z", "x", "y"))
COLUMNS = ((0, 256), (256, 256), (512, 640))
TN = 512
UNROLL = True


def mm(a, b):
    return lax.dot_general(a, b, (((1,), (0,)), ((), ())), preferred_element_type=f32)


def mm_nt(a, b):
    return lax.dot_general(a, b, (((1,), (1,)), ((), ())), preferred_element_type=f32)


def split2(v):
    hi = v.astype(bf16)
    return hi, (v - hi.astype(f32)).astype(bf16)


def iota(shape, dim):
    return lax.broadcasted_iota(jnp.int32, shape, dim)


def kernel(
    tok_hbm, w_hbm, head_hbm, seg_hbm, own_hbm, img_hbm, gain_hbm, lp_ref,
    loss_out, dtok_hbm, dw_out, dgain_out, dimg_out,
    tok, wv, headv, img, lcol, segt, invc, xs, xp, npst, pooled, asrc, arcv, tbuf, dcap, stack,
    seg_ref, own_ref, img_ref, gain_ref, stage, wh, coefs, zc, bacc, rsacc, c3as, c3ar, c3bs, c3br, gbuf, g2,
    ld_sem, w_sem, in_sem, st_sem,
    i_send, i_recv, j_send, j_recv, ic_send, ic_recv, t_send, t_recv, tc_send, tc_recv, a_send, a_recv,
    ca_send, ca_recv, cb_send, cb_recv, g_send, g_recv, h_send, h_recv,
):
    b = lax.axis_index("blk")
    d = lax.axis_index("dp")
    z, xh, core = b // 4, (b // 2) % 2, b % 2
    y, xl = d // 2, d % 2
    x = xh * 2 + xl
    sib = (b + 1 - 2 * core, d)

    here = {"x": x, "y": y, "z": z, "core": core}

    def device(at):
        return (at["z"] * 4 + (at["x"] // 2) * 2 + at["core"], at["y"] * 2 + at["x"] % 2)

    def step_of(axis, n):
        at = dict(here)
        at[axis] = (here[axis] + 4 + n) % 4
        return at

    barrier = pltpu.get_barrier_semaphore()
    pl.semaphore_signal(barrier, inc=1, device_id=sib, device_id_type=MESH)
    for axis in ("x", "y", "z"):
        for k in (1, 3, 2):
            pl.semaphore_signal(barrier, inc=1, device_id=device(step_of(axis, k)), device_id_type=MESH)

    inputs = []
    for i, (src, dst) in enumerate(((img_hbm, img_ref), (seg_hbm, seg_ref), (own_hbm, own_ref), (gain_hbm, gain_ref))):
        cp = pltpu.make_async_copy(src, dst, in_sem.at[i])
        cp.start()
        inputs.append(cp)
    loads = []
    for i in range(4):
        cp = pltpu.make_async_copy(
            tok_hbm.at[pl.ds(i * 128, 128), :], tok.at[pl.ds(i * 128, 128), :], ld_sem.at[i]
        )
        cp.start()
        loads.append(cp)
    wloads = []
    for i in range(DT // TN):
        cp = pltpu.make_async_copy(
            w_hbm.at[:, pl.ds(i * TN, TN)], wv.at[:, pl.ds(i * TN, TN)], w_sem.at[i]
        )
        cp.start()
        wloads.append(cp)
    hload = pltpu.make_async_copy(head_hbm, headv, ld_sem.at[4])
    hload.start()

    inputs[0].wait()
    im = img_ref[...].astype(f32)
    img_inv = lax.rsqrt(jnp.sum(im * im, axis=1, keepdims=True) + 1e-06)
    img_unit = im * img_inv
    img[z, xh, core, y, xl] = img_unit.astype(bf16)

    sends = []

    def region(p, at):
        def pick(name):
            return slice(None) if at[name] is None else at[name]

        xx = at["x"]
        return img.at[
            pick("z"),
            slice(None) if xx is None else xx // 2,
            at["core"],
            pick("y"),
            slice(None) if xx is None else xx % 2,
            :,
            pl.ds(*COLUMNS[p]),
        ]

    def ring_region(p, done, where):
        at = dict(where)
        for name in done:
            at[name] = None
        return region(p, at)

    def ring_copy(p, s, k, where, to):
        ref = ring_region(p, ORDERS[p][:s], where)
        return pltpu.make_async_remote_copy(
            src_ref=ref, dst_ref=ref, send_sem=i_send.at[p, s, k], recv_sem=i_recv.at[p, s, k],
            device_id=device(to), device_id_type=MESH,
        )

    def last_copy(p, j, k, where, to):
        first, second, _ = ORDERS[p]
        at = dict(where)
        at[second] = (here[second] + 4 - j) % 4
        ref = ring_region(p, (first,), at)
        return pltpu.make_async_remote_copy(
            src_ref=ref, dst_ref=ref, send_sem=j_send.at[p, j, k], recv_sem=j_recv.at[p, j, k],
            device_id=device(to), device_id_type=MESH,
        )

    def ring_send(p, s):
        for k in range(3):
            cp = ring_copy(p, s, k, here, step_of(ORDERS[p][s], k + 1))
            cp.start()
            sends.append(cp)

    def ring_wait(p, s, k):
        frm = step_of(ORDERS[p][s], -1 - k)
        ring_copy(p, s, k, frm, frm).wait_recv()

    def last_send(p, j):
        for k in range(3):
            cp = last_copy(p, j, k, here, step_of(ORDERS[p][2], k + 1))
            cp.start()
            sends.append(cp)

    def last_wait(p, k):
        frm = step_of(ORDERS[p][2], -1 - k)
        for j in range(4):
            last_copy(p, j, k, frm, frm).wait_recv()

    def core_copy(p, q, own):
        order = ORDERS[p]
        at = dict(here)
        for name in order[:2]:
            at[name] = None
        if q:
            at[order[2]] = (here[order[2]] + 4 - q) % 4
        if not own:
            at["core"] = 1 - core
        ref = region(p, at)
        return pltpu.make_async_remote_copy(
            src_ref=ref, dst_ref=ref, send_sem=ic_send.at[p, q], recv_sem=ic_recv.at[p, q],
            device_id=sib, device_id_type=MESH,
        )

    def core_send(p, q):
        cp = core_copy(p, q, True)
        cp.start()
        sends.append(cp)

    pl.semaphore_wait(barrier, 10)
    for p in range(PARTS):
        ring_send(p, 0)

    for cp in inputs[1:]:
        cp.wait()
    segf = seg_ref[...].astype(f32)
    segt[...] = jnp.broadcast_to(segf, (128, ROWS)).T
    lane = iota((128, 128), 1)
    cap_of = (lane % CAPS).astype(f32)
    kind = lane // CAPS

    def token_rows(i):
        loads[i].wait()
        rows = pl.ds(i * 128, 128)
        xx = tok[rows, :].astype(f32)
        inv = lax.rsqrt(jnp.sum(xx * xx, axis=1, keepdims=True) * (1.0 / DT) + 1e-06)
        invc[rows, :] = inv
        hi = inv.astype(bf16).astype(f32)
        lo = inv - hi
        val = jnp.where(kind == 0, 1.0, jnp.where(kind == 2, lo, hi))
        lcol[rows, :] = jnp.where(segt[rows, :] == cap_of, val, 0.0)

    for i in range(4):
        token_rows(i)

    lrow = lcol[...].T.astype(bf16)

    def pool_tile(i, _):
        cols = pl.ds(pl.multiple_of(i * TN, TN), TN)
        acc = mm(lrow, tok[:, cols])
        xs[:, cols] = acc[0:CAPS]
        xpt = acc[CAPS : 2 * CAPS] + acc[2 * CAPS : 3 * CAPS]
        xp[:, cols] = xpt
        hi, lo = split2(xpt * gain_ref[:, cols])
        npst[0:CAPS, cols] = hi
        npst[CAPS : 2 * CAPS, cols] = lo
        return 0

    lax.fori_loop(0, DT // TN, pool_tile, 0)

    sel = (jnp.broadcast_to(segf, (CAPS, ROWS)) == iota((CAPS, ROWS), 0).astype(f32)).astype(f32)
    rcount = 1.0 / jnp.maximum(jnp.sum(sel, axis=1, keepdims=True), 1.0)
    ownf = own_ref[...].astype(f32)
    own_col = jnp.sum(
        jnp.where(iota((CAPS, CAPS), 0) == iota((CAPS, CAPS), 1), jnp.broadcast_to(ownf, (CAPS, CAPS)), 0.0),
        axis=1,
        keepdims=True,
    )

    for i in range(DT // TN):
        if i == 2:
            for p in range(PARTS):
                for k in range(3):
                    ring_wait(p, 0, k)
                ring_send(p, 1)
                last_send(p, 0)
        wloads[i].wait()
        cols = pl.ds(i * TN, TN)
        yy = mm(npst[...], wv[:, cols])
        pooled[:, cols] = ((xs[:, cols] + yy[0:CAPS] + yy[CAPS : 2 * CAPS]) * rcount).astype(bf16)

    hload.wait()
    proj = mm(pooled[...], headv[...])
    scale_inv = lax.rsqrt(jnp.sum(proj * proj, axis=1, keepdims=True) + 1e-06)
    text_unit = proj * scale_inv
    text = text_unit.astype(bf16)
    tbuf[b, :, 0:E] = text
    tbuf[b, :, E:PW] = jnp.broadcast_to(own_col, (CAPS, 128)).astype(bf16)
    factor = scale_inv * rcount
    for j in range(NB):
        cols = pl.ds(j * 128, 128)
        asrc[j] = (xp[:, cols] * factor).astype(bf16)
    arcv[b] = asrc[b]

    def text_peer(k, sign):
        dz, dx = (k + 1) // 2, (k + 1) % 2
        return ((z + 4 + sign * dz) % 4) * 4 + ((xh + dx) % 2) * 2 + core

    def text_copy(k, idx, to):
        return pltpu.make_async_remote_copy(
            src_ref=tbuf.at[idx], dst_ref=tbuf.at[idx], send_sem=t_send.at[k], recv_sem=t_recv.at[k],
            device_id=(to, d), device_id_type=MESH,
        )

    def text_core(k, idx):
        return pltpu.make_async_remote_copy(
            src_ref=tbuf.at[idx], dst_ref=tbuf.at[idx], send_sem=tc_send.at[k], recv_sem=tc_recv.at[k],
            device_id=sib, device_id_type=MESH,
        )

    for k in range(7):
        cp = text_copy(k, b, text_peer(k, 1))
        cp.start()
        sends.append(cp)
    cp = text_core(7, b)
    cp.start()
    sends.append(cp)
    wh[...] = mm(wv[pl.ds(pl.multiple_of(b * 128, 128), 128), :], headv[...])

    for k in (0, 2, 1):
        for p in range(PARTS):
            ring_wait(p, 1, k)
            last_send(p, k + 1)
    for p in range(PARTS):
        core_send(p, 0)
    for k in range(NB - 1):
        to = (b + k + 1) % NB
        cp = pltpu.make_async_remote_copy(
            src_ref=asrc.at[to], dst_ref=arcv.at[b], send_sem=a_send.at[k], recv_sem=a_recv.at[k],
            device_id=(to, d), device_id_type=MESH,
        )
        cp.start()
        sends.append(cp)
    for k in range(7):
        frm = text_peer(k, -1)
        text_copy(k, frm, frm).wait_recv()
        cp = text_core(k, frm)
        cp.start()
        sends.append(cp)
    for k in (0, 2, 1):
        for p in range(PARTS):
            last_wait(p, k)
            core_send(p, k + 1)
    for p in range(PARTS):
        for q in range(4):
            core_copy(p, q, False).wait_recv()

    scale = jnp.exp(jnp.full((1, 128), lp_ref[0], f32))[:, 0:1]
    bias = jnp.full((1, 128), lp_ref[1], f32)[:, 0:1]

    def pair(dots, gid, first):
        ids = (iota((1, dots.shape[1]), 1) + first).astype(f32)
        val = scale * dots + bias
        same = gid == ids
        arg = jnp.where(same, -val, val)
        coef = jnp.where(same, -scale, scale) * pl.reciprocal(1.0 + jnp.exp(-arg), approx=True)
        return arg, coef

    def dp_copy(buf, src, idx, k, ssem, rsem):
        return pltpu.make_async_remote_copy(
            src_ref=src, dst_ref=buf.at[idx], send_sem=ssem.at[k], recv_sem=rsem.at[k],
            device_id=(b, (d + k + 1) % ND), device_id_type=MESH,
        )

    def dp_wait(buf, k, ssem, rsem):
        frm = (d + ND - 1 - k) % ND
        dp_copy(buf, buf.at[frm], frm, k, ssem, rsem).wait_recv()

    for k in range(7):
        frm = text_peer(k, -1)
        text_core(k, frm + 1 - 2 * core).wait_recv()
    text_core(7, sib[0]).wait_recv()

    slots = NB * CAPS
    owner = tbuf[:, :, E:PW].reshape(slots, 128).astype(f32)[:, 0:1]
    block = (iota((slots, 1), 0) // CAPS * 128).astype(f32)
    gid = jnp.where(owner >= 0.0, owner + block, -1.0)
    texts = tbuf[:, :, 0:E].reshape(slots, E)
    group = img[z, xh, core].reshape(128, E)
    arg, coef = pair(mm_nt(texts, group), gid, b * 128)
    dimg_part = mm(coef.T.astype(bf16), texts)
    c3as[...] = dimg_part.reshape(ND, 16, E).astype(bf16)
    c3ar[d] = c3as[d]
    for k in range(ND - 1):
        cp = dp_copy(c3ar, c3as.at[(d + k + 1) % ND], d, k, ca_send, ca_recv)
        cp.start()
        sends.append(cp)
    soft = jnp.maximum(arg, 0.0) + jnp.log1p(jnp.exp(-jnp.abs(arg)))
    loss_part = jnp.sum(jnp.where(gid >= 0.0, soft, 0.0), axis=0, keepdims=True)

    for k in range(NB - 1):
        frm = (b + NB - 1 - k) % NB
        pltpu.make_async_remote_copy(
            src_ref=arcv.at[frm], dst_ref=arcv.at[frm], send_sem=a_send.at[k], recv_sem=a_recv.at[k],
            device_id=(frm, d), device_id_type=MESH,
        ).wait_recv()
    share = arcv[...].reshape(slots, 128).astype(f32)
    share_t = share.T.astype(bf16)
    bacc[...] = jnp.zeros((128 + CAPS, E), f32)
    rsacc[...] = jnp.zeros((slots, 1), f32)

    def pair_chunk(c, _):
        chunk = img[c].reshape(512, E)
        dots = mm_nt(tbuf[:, :, 0:E].reshape(slots, E), chunk)
        _, coef = pair(dots, gid, c * 512)
        rsacc[...] += jnp.sum(coef * dots, axis=1, keepdims=True)
        coefs[...] = coef.astype(bf16)
        zc[0:128, :] = mm(share_t, coefs[...]).astype(bf16)
        zc[128 : 128 + CAPS, :] = coefs[pl.ds(pl.multiple_of(b * CAPS, CAPS), CAPS), :]
        bacc[...] += mm(zc[...], chunk)
        return 0

    lax.fori_loop(0, 4, pair_chunk, 0, unroll=UNROLL)

    minus_t = (share * rsacc[...]).T.astype(bf16)
    bpart = bacc[0:128, :] - mm(minus_t, texts)
    c3bs[...] = bpart.reshape(ND, 16, E).astype(bf16)
    c3br[d] = c3bs[d]
    gain_part = jnp.sum(bpart * wh[...], axis=1, keepdims=True)
    gbuf[d, 0:8, :] = jnp.broadcast_to(loss_part, (8, 128))
    gbuf[d, 8:16, :] = jnp.broadcast_to(gain_part, (128, 128)).T[0:8]
    for k in range(ND - 1):
        cp = dp_copy(gbuf, gbuf.at[d], d, k, g_send, g_recv)
        cp.start()
        sends.append(cp)
    for k in range(ND - 1):
        cp = dp_copy(c3br, c3bs.at[(d + k + 1) % ND], d, k, cb_send, cb_recv)
        cp.start()
        sends.append(cp)

    dtext = bacc[128 : 128 + CAPS, :]
    dproj = (
        scale_inv * (dtext - text_unit * jnp.sum(text_unit * dtext, axis=1, keepdims=True))
    ).astype(bf16)
    live = jnp.where(own_col >= 0.0, rcount, 0.0)

    def dcap_tile(i, _):
        rows = pl.ds(pl.multiple_of(i * TN, TN), TN)
        dpool = mm_nt(dproj, headv[rows, :]).astype(bf16).astype(f32)
        dc = (dpool * live).astype(bf16)
        dcap[:, rows] = dc
        stack[0:CAPS, rows] = dc
        return 0

    lax.fori_loop(0, DT // TN, dcap_tile, 0)

    for k in range(ND - 1):
        dp_wait(gbuf, k, g_send, g_recv)
    gsum = jnp.sum(gbuf[...], axis=0)
    g2[b] = gsum[8:16]
    for k in range(NB - 1):
        cp = pltpu.make_async_remote_copy(
            src_ref=g2.at[b], dst_ref=g2.at[b], send_sem=h_send.at[k], recv_sem=h_recv.at[k],
            device_id=((b + k + 1) % NB, d), device_id_type=MESH,
        )
        cp.start()
        sends.append(cp)

    def dnorm_tile(i, _):
        rows = pl.ds(pl.multiple_of(i * TN, TN), TN)
        hi, lo = split2(mm_nt(dcap[...], wv[rows, :]) * gain_ref[:, rows])
        stack[CAPS : 2 * CAPS, rows] = hi
        stack[2 * CAPS : 3 * CAPS, rows] = hi
        stack[3 * CAPS : 4 * CAPS, rows] = lo
        return 0

    lax.fori_loop(0, DT // TN, dnorm_tile, 0)

    stores = []
    for i in range(4):
        rows = pl.ds(i * 128, 128)
        xb = tok[rows, :]
        lc = lcol[rows, :]
        q = mm_nt(xb, stack[...])
        mine = (segt[rows, :] == cap_of) & ((kind == 1) | (kind == 3))
        mean = jnp.sum(jnp.where(mine, q, 0.0), axis=1, keepdims=True) * (1.0 / DT)
        inv = invc[rows, :]
        drop = inv * inv * inv * mean
        full = mm(lc.astype(bf16), stack[...])
        stage[rows, :] = (full - xb.astype(f32) * drop).astype(bf16)
        cp = pltpu.make_async_copy(stage.at[rows, :], dtok_hbm.at[rows, :], st_sem.at[i])
        cp.start()
        stores.append(cp)

    for k in range(ND - 1):
        dp_wait(c3ar, k, ca_send, ca_recv)
    dimg = jnp.sum(c3ar[...].astype(f32), axis=0)
    dimg_out[...] = img_inv * (dimg - img_unit * jnp.sum(img_unit * dimg, axis=1, keepdims=True))
    for k in range(ND - 1):
        dp_wait(c3br, k, cb_send, cb_recv)
    mine = iota((16, 128), 1) == iota((16, 128), 0) + 16 * d

    def own_rows(row):
        return jnp.sum(jnp.where(mine, jnp.broadcast_to(row, (16, 128)), 0.0), axis=1, keepdims=True)

    gain_col = own_rows(gain_ref[:, pl.ds(pl.multiple_of(b * 128, 128), 128)])
    hi, lo = split2(jnp.sum(c3br[...].astype(f32), axis=0) * gain_col)
    both = jnp.concatenate([hi, lo], axis=0)

    def dw_tile(i, _):
        rows = pl.ds(pl.multiple_of(i * TN, TN), TN)
        dw = mm_nt(both, headv[rows, :])
        dw_out[:, rows] = dw[0:16] + dw[16:32]
        return 0

    lax.fori_loop(0, DT // TN, dw_tile, 0)

    col = own_rows(gsum[0:1] * (1.0 / TOTAL))
    loss_out[...] = jnp.sum(jnp.where(iota((16, 16), 0) == iota((16, 16), 1), col, 0.0), axis=0, keepdims=True)

    for k in range(NB - 1):
        frm = (b + NB - 1 - k) % NB
        pltpu.make_async_remote_copy(
            src_ref=g2.at[frm], dst_ref=g2.at[frm], send_sem=h_send.at[k], recv_sem=h_recv.at[k],
            device_id=(frm, d), device_id_type=MESH,
        ).wait_recv()
    for r in range(NB):
        dgain_out[r : r + 1, :] = g2[r, 0:1, :]

    for cp in stores:
        cp.wait()
    for cp in sends:
        cp.wait_send()


def hand_over(loss, dtok, dw, dgain, dimg, loss_out, dtok_out, dw_out, dgain_out, dimg_out, buf, ins, outs):
    reads = []
    for i in range(4):
        cp = pltpu.make_async_copy(dtok.at[pl.ds(i * 128, 128), :], buf.at[pl.ds(i * 128, 128), :], ins.at[i])
        cp.start()
        reads.append(cp)
    loss_out[...] = loss[...]
    dw_out[...] = dw[...]
    dgain_out[...] = dgain[...]
    dimg_out[...] = dimg[...]
    writes = []
    for i in range(4):
        reads[i].wait()
        cp = pltpu.make_async_copy(buf.at[pl.ds(i * 128, 128), :], dtok_out.at[pl.ds(i * 128, 128), :], outs.at[i])
        cp.start()
        writes.append(cp)
    for cp in writes:
        cp.wait()


def per_device(tokens, segment_ids, owners, images, weight, gain, head, logit_params):
    vmem = pl.BlockSpec(memory_space=pltpu.VMEM)
    hbm = pl.BlockSpec(memory_space=pl.ANY)
    dma = pltpu.SemaphoreType.DMA
    shapes = (
        jax.ShapeDtypeStruct((1, 16), f32),
        jax.ShapeDtypeStruct((ROWS, DT), bf16),
        jax.ShapeDtypeStruct((16, DT), f32),
        jax.ShapeDtypeStruct((16, 128), f32),
        jax.ShapeDtypeStruct((16, E), f32),
    )
    held = pl.pallas_call(
        kernel,
        out_shape=shapes,
        in_specs=[hbm, hbm, hbm, hbm, hbm, hbm, hbm, pl.BlockSpec(memory_space=pltpu.SMEM)],
        out_specs=(vmem, hbm, vmem, vmem, vmem),
        scratch_shapes=[
            pltpu.VMEM((ROWS, DT), bf16),
            pltpu.VMEM((DT, DT), bf16),
            pltpu.VMEM((DT, E), bf16),
            pltpu.VMEM((4, 2, 2, 4, 2, 16, E), bf16),
            pltpu.VMEM((ROWS, 128), f32),
            pltpu.VMEM((ROWS, 128), f32),
            pltpu.VMEM((ROWS, 1), f32),
            pltpu.VMEM((CAPS, DT), f32),
            pltpu.VMEM((CAPS, DT), f32),
            pltpu.VMEM((2 * CAPS, DT), bf16),
            pltpu.VMEM((CAPS, DT), bf16),
            pltpu.VMEM((NB, CAPS, 128), bf16),
            pltpu.VMEM((NB, CAPS, 128), bf16),
            pltpu.VMEM((NB, CAPS, PW), bf16),
            pltpu.VMEM((CAPS, DT), bf16),
            pltpu.VMEM((4 * CAPS, DT), bf16),
            pltpu.VMEM((1, ROWS), jnp.int32),
            pltpu.VMEM((1, CAPS), jnp.int32),
            pltpu.VMEM((16, E), bf16),
            pltpu.VMEM((1, DT), f32),
            pltpu.VMEM((ROWS, DT), bf16),
            pltpu.VMEM((128, E), f32),
            pltpu.VMEM((NB * CAPS, 512), bf16),
            pltpu.VMEM((128 + CAPS, 512), bf16),
            pltpu.VMEM((128 + CAPS, E), f32),
            pltpu.VMEM((NB * CAPS, 1), f32),
            pltpu.VMEM((ND, 16, E), bf16),
            pltpu.VMEM((ND, 16, E), bf16),
            pltpu.VMEM((ND, 16, E), bf16),
            pltpu.VMEM((ND, 16, E), bf16),
            pltpu.VMEM((ND, 16, 128), f32),
            pltpu.VMEM((NB, 8, 128), f32),
            dma((5,)),
            dma((DT // TN,)),
            dma((4,)),
            dma((4,)),
            dma((PARTS, 2, 3)),
            dma((PARTS, 2, 3)),
            dma((PARTS, 4, 3)),
            dma((PARTS, 4, 3)),
            dma((PARTS, 4)),
            dma((PARTS, 4)),
            dma((7,)),
            dma((7,)),
            dma((8,)),
            dma((8,)),
            dma((NB - 1,)),
            dma((NB - 1,)),
            dma((ND - 1,)),
            dma((ND - 1,)),
            dma((ND - 1,)),
            dma((ND - 1,)),
            dma((ND - 1,)),
            dma((ND - 1,)),
            dma((NB - 1,)),
            dma((NB - 1,)),
        ],
        compiler_params=pltpu.CompilerParams(
            collective_id=0, has_side_effects=True, vmem_limit_bytes=56 * 1024 * 1024
        ),
    )(tokens, weight, head, segment_ids, owners, images, gain.reshape(1, DT), logit_params)
    loss, d_tokens, d_weight, d_gain, d_images = pl.pallas_call(
        hand_over,
        out_shape=shapes,
        in_specs=[vmem, hbm, vmem, vmem, vmem],
        out_specs=(vmem, hbm, vmem, vmem, vmem),
        scratch_shapes=[pltpu.VMEM((ROWS, DT), bf16), dma((4,)), dma((4,))],
        compiler_params=pltpu.CompilerParams(vmem_limit_bytes=56 * 1024 * 1024),
    )(*held)
    return loss.reshape(16), d_tokens, d_weight, d_gain.reshape(DT), d_images


def solution(mesh):
    rows = P(("blk", "dp"), None)
    return jax.shard_map(
        per_device,
        mesh=mesh,
        in_specs=(rows, rows, rows, rows, P(), P(), P(), P()),
        out_specs=(P(("blk", "dp")), rows, rows, P(), rows),
        check_vma=False,
    )
```

time: 72.3 us -> 61.7 us (0.85)
  local copies, waits for them, and re-layouts: 6.28 us -> 0 us
  Pallas kernels: 65.2 us -> 60.9 us
    unnamed x11 -> x0, local copies, waits for them, and re-layouts: 6.28 us -> none
    pallas_call x1 -> x2, Pallas kernels: 65.2 us -> 60.9 us  [the longest x1 56.8 us: per_device(): pl.pallas_call(kernel, out_shape=shapes, in_specs=[hbm, hbm, hbm, hbm, hb...]
where the time goes in v2:
time: 61.7 us; the launch traced here: 61.6 us
  Pallas kernels  60.9 us (99%)
  between operations  0.64 us (1%)
    pallas_call x1, Pallas kernels, per_device(): pl.pallas_call(kernel, out_shape=shapes, in_specs=[hbm, hbm, hbm, hbm, hb...  56.8 us
    pallas_call x1, Pallas kernels, per_device(): pl.pallas_call(hand_over, out_shape=shapes, in_specs=[vmem, hbm, vmem, vm...  4.08 us

profile of v2, /device:TPU:1, one launch (start us, length us, event | category | flops | bytes accessed | tf_op | source)
XLA Modules:
  0.0 61.6 jit_solution(16266747576561322360)
XLA Ops:
  0.6 56.8 %shard_map.119 = (f32[1,16]{1,0:T(1,128)}, bf16[512,2048]{1,0:T(8,128)(2,1)}, f32[16,2048]{1,0:T(8,128)}, f32[16,128]{1,0:T(8,128)}, f32[16,1152]{1,0:T(8,128)}) custom-call(bf16[512,2048]{1,0:T(8,128)(2,1)} %tok_hbm.1, bf16[2048,2048]{1,0:T(8,128)(2,1)} %w_hbm.1, bf16[2048,1152]{1,0:T(8,128)(2,1)} %head_hbm.1, s32[1,512]{1,0:T(1,128)} %seg_hbm.1, ...), custom_call_target="tpu_custom_call" | custom-call | tf_op jit(solution)/shard_map/pallas_call | solution.py:524
  57.5 4.1 %shard_map.120 = (f32[1,16]{1,0:T(1,128)}, bf16[512,2048]{1,0:T(8,128)(2,1)}, f32[16,2048]{1,0:T(8,128)}, f32[16,128]{1,0:T(8,128)}, f32[16,1152]{1,0:T(8,128)}) custom-call(f32[1,16]{1,0:T(1,128)} %get-tuple-element.15.loss, bf16[512,2048]{1,0:T(8,128)(2,1)} %get-tuple-element.16.dtok, f32[16,2048]{1,0:T(8,128)} %get-tuple-element.17.dw, ...), custom_call_target="tpu_custom_call" | custom-call | tf_op jit(solution)/shard_map/pallas_call | solution.py:591

commit v3 on v2

--- a/solution.py
+++ b/solution.py
@@ -18,10 +18,14 @@
 NB = 16
 ND = 8
 TOTAL = 2048
+NC = 8
+NR = 16
+SLOTS = NC * CAPS
+GR = NR * 16
 PW = E + 128
 PARTS = 3
 ORDERS = (("x", "y", "z"), ("y", "z", "x"), ("z", "x", "y"))
-COLUMNS = ((0, 256), (256, 256), (512, 640))
+COLUMNS = ((0, 256), (256, 384), (640, 512))
 TN = 512
 UNROLL = True
 
@@ -58,6 +62,8 @@
     y, xl = d // 2, d % 2
     x = xh * 2 + xl
     sib = (b + 1 - 2 * core, d)
+    place = z * 2 + core
+    seat = xh * ND + d
 
     here = {"x": x, "y": y, "z": z, "core": core}
 
@@ -251,22 +257,18 @@
     scale_inv = lax.rsqrt(jnp.sum(proj * proj, axis=1, keepdims=True) + 1e-06)
     text_unit = proj * scale_inv
     text = text_unit.astype(bf16)
-    tbuf[b, :, 0:E] = text
-    tbuf[b, :, E:PW] = jnp.broadcast_to(own_col, (CAPS, 128)).astype(bf16)
+    tbuf[place, :, 0:E] = text
+    tbuf[place, :, E:PW] = jnp.broadcast_to(own_col, (CAPS, 128)).astype(bf16)
     factor = scale_inv * rcount
     for j in range(NB):
         cols = pl.ds(j * 128, 128)
-        asrc[j] = (xp[:, cols] * factor).astype(bf16)
-    arcv[b] = asrc[b]
-
-    def text_peer(k, sign):
-        dz, dx = (k + 1) // 2, (k + 1) % 2
-        return ((z + 4 + sign * dz) % 4) * 4 + ((xh + dx) % 2) * 2 + core
+        asrc[j // 4 * 2 + j % 2, j // 2 % 2] = (xp[:, cols] * factor).astype(bf16)
+    arcv[place] = asrc[place]
 
     def text_copy(k, idx, to):
         return pltpu.make_async_remote_copy(
             src_ref=tbuf.at[idx], dst_ref=tbuf.at[idx], send_sem=t_send.at[k], recv_sem=t_recv.at[k],
-            device_id=(to, d), device_id_type=MESH,
+            device_id=device(to), device_id_type=MESH,
         )
 
     def text_core(k, idx):
@@ -275,33 +277,47 @@
             device_id=sib, device_id_type=MESH,
         )
 
-    for k in range(7):
-        cp = text_copy(k, b, text_peer(k, 1))
-        cp.start()
-        sends.append(cp)
-    cp = text_core(7, b)
+    for k in range(3):
+        cp = text_copy(k, place, step_of("z", k + 1))
+        cp.start()
+        sends.append(cp)
+    cp = text_core(3, place)
     cp.start()
     sends.append(cp)
-    wh[...] = mm(wv[pl.ds(pl.multiple_of(b * 128, 128), 128), :], headv[...])
-
     for k in (0, 2, 1):
         for p in range(PARTS):
             ring_wait(p, 1, k)
             last_send(p, k + 1)
     for p in range(PARTS):
         core_send(p, 0)
-    for k in range(NB - 1):
-        to = (b + k + 1) % NB
-        cp = pltpu.make_async_remote_copy(
-            src_ref=asrc.at[to], dst_ref=arcv.at[b], send_sem=a_send.at[k], recv_sem=a_recv.at[k],
-            device_id=(to, d), device_id_type=MESH,
-        )
-        cp.start()
-        sends.append(cp)
-    for k in range(7):
-        frm = text_peer(k, -1)
-        text_copy(k, frm, frm).wait_recv()
-        cp = text_core(k, frm)
+
+    def column_peer(k):
+        n = (place + k + 1) % NC
+        return n, (n // 2 * 4 + xh * 2 + n % 2, d)
+
+    def column_copy(src, dst, k, to, ssem, rsem):
+        return pltpu.make_async_remote_copy(
+            src_ref=src, dst_ref=dst, send_sem=ssem.at[k], recv_sem=rsem.at[k], device_id=to, device_id_type=MESH
+        )
+
+    def column_wait(buf, k, ssem, rsem):
+        frm, dev = column_peer(NC - 2 - k)
+        column_copy(buf.at[frm], buf.at[frm], k, dev, ssem, rsem).wait_recv()
+
+    for k in range(NC - 1):
+        n, to = column_peer(k)
+        cp = column_copy(asrc.at[n], arcv.at[place], k, to, a_send, a_recv)
+        cp.start()
+        sends.append(cp)
+    first = pl.multiple_of((z * 4 + core) * 128, 128)
+    rows_of = [wv[pl.ds(pl.multiple_of(first + 256 * h, 128), 128), :] for h in range(2)]
+    wh[...] = mm(jnp.concatenate(rows_of, axis=0), headv[...])
+
+    for k in (0, 2, 1):
+        frm = step_of("z", -1 - k)
+        idx = frm["z"] * 2 + core
+        text_copy(k, idx, frm).wait_recv()
+        cp = text_core(k, idx)
         cp.start()
         sends.append(cp)
     for k in (0, 2, 1):
@@ -315,87 +331,86 @@
     scale = jnp.exp(jnp.full((1, 128), lp_ref[0], f32))[:, 0:1]
     bias = jnp.full((1, 128), lp_ref[1], f32)[:, 0:1]
 
-    def pair(dots, gid, first):
-        ids = (iota((1, dots.shape[1]), 1) + first).astype(f32)
+    def pair(dots, gid, ids):
         val = scale * dots + bias
         same = gid == ids
         arg = jnp.where(same, -val, val)
         coef = jnp.where(same, -scale, scale) * pl.reciprocal(1.0 + jnp.exp(-arg), approx=True)
         return arg, coef
 
-    def dp_copy(buf, src, idx, k, ssem, rsem):
+    def row_copy(src, dst, k, ssem, rsem):
+        n = (seat + k + 1) % NR
         return pltpu.make_async_remote_copy(
-            src_ref=src, dst_ref=buf.at[idx], send_sem=ssem.at[k], recv_sem=rsem.at[k],
-            device_id=(b, (d + k + 1) % ND), device_id_type=MESH,
-        )
-
-    def dp_wait(buf, k, ssem, rsem):
-        frm = (d + ND - 1 - k) % ND
-        dp_copy(buf, buf.at[frm], frm, k, ssem, rsem).wait_recv()
-
-    for k in range(7):
-        frm = text_peer(k, -1)
-        text_core(k, frm + 1 - 2 * core).wait_recv()
-    text_core(7, sib[0]).wait_recv()
-
-    slots = NB * CAPS
-    owner = tbuf[:, :, E:PW].reshape(slots, 128).astype(f32)[:, 0:1]
-    block = (iota((slots, 1), 0) // CAPS * 128).astype(f32)
+            src_ref=src, dst_ref=dst, send_sem=ssem.at[k], recv_sem=rsem.at[k],
+            device_id=(z * 4 + n // ND * 2 + core, n % ND), device_id_type=MESH,
+        )
+
+    def row_wait(buf, k, ssem, rsem):
+        frm = (seat + NR - 1 - k) % NR
+        row_copy(buf.at[frm], buf.at[frm], k, ssem, rsem).wait_recv()
+
+    for k in (0, 2, 1):
+        text_core(k, step_of("z", -1 - k)["z"] * 2 + 1 - core).wait_recv()
+    text_core(3, place + 1 - 2 * core).wait_recv()
+
+    owner = tbuf[:, :, E:PW].reshape(SLOTS, 128).astype(f32)[:, 0:1]
+    row = iota((SLOTS, 1), 0) // CAPS
+    block = ((row // 2 * 4 + row % 2 + xh * 2) * 128).astype(f32)
     gid = jnp.where(owner >= 0.0, owner + block, -1.0)
-    texts = tbuf[:, :, 0:E].reshape(slots, E)
-    group = img[z, xh, core].reshape(128, E)
-    arg, coef = pair(mm_nt(texts, group), gid, b * 128)
+    texts = tbuf[:, :, 0:E].reshape(SLOTS, E)
+    group = img[z, :, core].reshape(GR, E)
+    lane_g = iota((1, GR), 1)
+    ids_g = ((z * 4 + core) * 128 + lane_g + lane_g // 128 * 128).astype(f32)
+    arg, coef = pair(mm_nt(texts, group), gid, ids_g)
     dimg_part = mm(coef.T.astype(bf16), texts)
-    c3as[...] = dimg_part.reshape(ND, 16, E).astype(bf16)
-    c3ar[d] = c3as[d]
-    for k in range(ND - 1):
-        cp = dp_copy(c3ar, c3as.at[(d + k + 1) % ND], d, k, ca_send, ca_recv)
+    c3as[...] = dimg_part.reshape(NR, 16, E).astype(bf16)
+    c3ar[seat] = c3as[seat]
+    for k in range(NR - 1):
+        cp = row_copy(c3as.at[(seat + k + 1) % NR], c3ar.at[seat], k, ca_send, ca_recv)
         cp.start()
         sends.append(cp)
     soft = jnp.maximum(arg, 0.0) + jnp.log1p(jnp.exp(-jnp.abs(arg)))
     loss_part = jnp.sum(jnp.where(gid >= 0.0, soft, 0.0), axis=0, keepdims=True)
 
-    for k in range(NB - 1):
-        frm = (b + NB - 1 - k) % NB
-        pltpu.make_async_remote_copy(
-            src_ref=arcv.at[frm], dst_ref=arcv.at[frm], send_sem=a_send.at[k], recv_sem=a_recv.at[k],
-            device_id=(frm, d), device_id_type=MESH,
-        ).wait_recv()
-    share = arcv[...].reshape(slots, 128).astype(f32)
+    for k in range(NC - 1):
+        column_wait(arcv, k, a_send, a_recv)
+    share = jnp.concatenate([arcv[:, h].reshape(SLOTS, 128) for h in range(2)], axis=1).astype(f32)
     share_t = share.T.astype(bf16)
-    bacc[...] = jnp.zeros((128 + CAPS, E), f32)
-    rsacc[...] = jnp.zeros((slots, 1), f32)
+    bacc[...] = jnp.zeros((GR + CAPS, E), f32)
+    rsacc[...] = jnp.zeros((SLOTS, 1), f32)
 
     def pair_chunk(c, _):
         chunk = img[c].reshape(512, E)
-        dots = mm_nt(tbuf[:, :, 0:E].reshape(slots, E), chunk)
-        _, coef = pair(dots, gid, c * 512)
+        dots = mm_nt(tbuf[:, :, 0:E].reshape(SLOTS, E), chunk)
+        _, coef = pair(dots, gid, (iota((1, 512), 1) + c * 512).astype(f32))
         rsacc[...] += jnp.sum(coef * dots, axis=1, keepdims=True)
         coefs[...] = coef.astype(bf16)
-        zc[0:128, :] = mm(share_t, coefs[...]).astype(bf16)
-        zc[128 : 128 + CAPS, :] = coefs[pl.ds(pl.multiple_of(b * CAPS, CAPS), CAPS), :]
+        zc[0:GR, :] = mm(share_t, coefs[...]).astype(bf16)
+        zc[GR : GR + CAPS, :] = coefs[pl.ds(pl.multiple_of(place * CAPS, CAPS), CAPS), :]
         bacc[...] += mm(zc[...], chunk)
         return 0
 
     lax.fori_loop(0, 4, pair_chunk, 0, unroll=UNROLL)
 
     minus_t = (share * rsacc[...]).T.astype(bf16)
-    bpart = bacc[0:128, :] - mm(minus_t, texts)
-    c3bs[...] = bpart.reshape(ND, 16, E).astype(bf16)
-    c3br[d] = c3bs[d]
-    gain_part = jnp.sum(bpart * wh[...], axis=1, keepdims=True)
-    gbuf[d, 0:8, :] = jnp.broadcast_to(loss_part, (8, 128))
-    gbuf[d, 8:16, :] = jnp.broadcast_to(gain_part, (128, 128)).T[0:8]
-    for k in range(ND - 1):
-        cp = dp_copy(gbuf, gbuf.at[d], d, k, g_send, g_recv)
-        cp.start()
-        sends.append(cp)
-    for k in range(ND - 1):
-        cp = dp_copy(c3br, c3bs.at[(d + k + 1) % ND], d, k, cb_send, cb_recv)
-        cp.start()
-        sends.append(cp)
-
-    dtext = bacc[128 : 128 + CAPS, :]
+    bpart = bacc[0:GR, :] - mm(minus_t, texts)
+    c3bs[...] = bpart.reshape(NR, 16, E).astype(bf16)
+    c3br[seat] = c3bs[seat]
+    gain_part = jnp.broadcast_to(jnp.sum(bpart * wh[...], axis=1, keepdims=True), (GR, 128)).T[0:1]
+    gbuf[seat] = jnp.zeros((8, 128), f32)
+    for h in range(2):
+        gbuf[seat, h : h + 1, :] = loss_part[:, 128 * h : 128 * h + 128]
+        gbuf[seat, 2 + h : 3 + h, :] = gain_part[:, 128 * h : 128 * h + 128]
+    for k in range(NR - 1):
+        cp = row_copy(gbuf.at[seat], gbuf.at[seat], k, g_send, g_recv)
+        cp.start()
+        sends.append(cp)
+    for k in range(NR - 1):
+        cp = row_copy(c3bs.at[(seat + k + 1) % NR], c3br.at[seat], k, cb_send, cb_recv)
+        cp.start()
+        sends.append(cp)
+
+    dtext = bacc[GR : GR + CAPS, :]
     dproj = (
         scale_inv * (dtext - text_unit * jnp.sum(text_unit * dtext, axis=1, keepdims=True))
     ).astype(bf16)
@@ -411,15 +426,13 @@
 
     lax.fori_loop(0, DT // TN, dcap_tile, 0)
 
-    for k in range(ND - 1):
-        dp_wait(gbuf, k, g_send, g_recv)
+    for k in range(NR - 1):
+        row_wait(gbuf, k, g_send, g_recv)
     gsum = jnp.sum(gbuf[...], axis=0)
-    g2[b] = gsum[8:16]
-    for k in range(NB - 1):
-        cp = pltpu.make_async_remote_copy(
-            src_ref=g2.at[b], dst_ref=g2.at[b], send_sem=h_send.at[k], recv_sem=h_recv.at[k],
-            device_id=((b + k + 1) % NB, d), device_id_type=MESH,
-        )
+    g2[place] = gsum
+    for k in range(NC - 1):
+        _, to = column_peer(k)
+        cp = column_copy(g2.at[place], g2.at[place], k, to, h_send, h_recv)
         cp.start()
         sends.append(cp)
 
@@ -449,12 +462,12 @@
         cp.start()
         stores.append(cp)
 
-    for k in range(ND - 1):
-        dp_wait(c3ar, k, ca_send, ca_recv)
+    for k in range(NR - 1):
+        row_wait(c3ar, k, ca_send, ca_recv)
     dimg = jnp.sum(c3ar[...].astype(f32), axis=0)
     dimg_out[...] = img_inv * (dimg - img_unit * jnp.sum(img_unit * dimg, axis=1, keepdims=True))
-    for k in range(ND - 1):
-        dp_wait(c3br, k, cb_send, cb_recv)
+    for k in range(NR - 1):
+        row_wait(c3br, k, cb_send, cb_recv)
     mine = iota((16, 128), 1) == iota((16, 128), 0) + 16 * d
 
     def own_rows(row):
@@ -472,17 +485,14 @@
 
     lax.fori_loop(0, DT // TN, dw_tile, 0)
 
-    col = own_rows(gsum[0:1] * (1.0 / TOTAL))
+    col = own_rows(jnp.where(xh == 0, gsum[0:1], gsum[1:2]) * (1.0 / TOTAL))
     loss_out[...] = jnp.sum(jnp.where(iota((16, 16), 0) == iota((16, 16), 1), col, 0.0), axis=0, keepdims=True)
 
-    for k in range(NB - 1):
-        frm = (b + NB - 1 - k) % NB
-        pltpu.make_async_remote_copy(
-            src_ref=g2.at[frm], dst_ref=g2.at[frm], send_sem=h_send.at[k], recv_sem=h_recv.at[k],
-            device_id=(frm, d), device_id_type=MESH,
-        ).wait_recv()
+    for k in range(NC - 1):
+        column_wait(g2, k, h_send, h_recv)
     for r in range(NB):
-        dgain_out[r : r + 1, :] = g2[r, 0:1, :]
+        h = r // 2 % 2
+        dgain_out[r : r + 1, :] = g2[r // 4 * 2 + r % 2, 2 + h : 3 + h, :]
 
     for cp in stores:
         cp.wait()
@@ -538,9 +548,9 @@
             pltpu.VMEM((CAPS, DT), f32),
             pltpu.VMEM((2 * CAPS, DT), bf16),
             pltpu.VMEM((CAPS, DT), bf16),
-            pltpu.VMEM((NB, CAPS, 128), bf16),
-            pltpu.VMEM((NB, CAPS, 128), bf16),
-            pltpu.VMEM((NB, CAPS, PW), bf16),
+            pltpu.VMEM((NC, 2, CAPS, 128), bf16),
+            pltpu.VMEM((NC, 2, CAPS, 128), bf16),
+            pltpu.VMEM((NC, CAPS, PW), bf16),
             pltpu.VMEM((CAPS, DT), bf16),
             pltpu.VMEM((4 * CAPS, DT), bf16),
             pltpu.VMEM((1, ROWS), jnp.int32),
@@ -548,17 +558,17 @@
             pltpu.VMEM((16, E), bf16),
             pltpu.VMEM((1, DT), f32),
             pltpu.VMEM((ROWS, DT), bf16),
-            pltpu.VMEM((128, E), f32),
-            pltpu.VMEM((NB * CAPS, 512), bf16),
-            pltpu.VMEM((128 + CAPS, 512), bf16),
-            pltpu.VMEM((128 + CAPS, E), f32),
-            pltpu.VMEM((NB * CAPS, 1), f32),
-            pltpu.VMEM((ND, 16, E), bf16),
-            pltpu.VMEM((ND, 16, E), bf16),
-            pltpu.VMEM((ND, 16, E), bf16),
-            pltpu.VMEM((ND, 16, E), bf16),
-            pltpu.VMEM((ND, 16, 128), f32),
-            pltpu.VMEM((NB, 8, 128), f32),
+            pltpu.VMEM((GR, E), f32),
+            pltpu.VMEM((SLOTS, 512), bf16),
+            pltpu.VMEM((GR + CAPS, 512), bf16),
+            pltpu.VMEM((GR + CAPS, E), f32),
+            pltpu.VMEM((SLOTS, 1), f32),
+            pltpu.VMEM((NR, 16, E), bf16),
+            pltpu.VMEM((NR, 16, E), bf16),
+            pltpu.VMEM((NR, 16, E), bf16),
+            pltpu.VMEM((NR, 16, E), bf16),
+            pltpu.VMEM((NR, 8, 128), f32),
+            pltpu.VMEM((NC, 8, 128), f32),
             dma((5,)),
             dma((DT // TN,)),
             dma((4,)),
@@ -569,20 +579,20 @@
             dma((PARTS, 4, 3)),
             dma((PARTS, 4)),
             dma((PARTS, 4)),
-            dma((7,)),
-            dma((7,)),
-            dma((8,)),
-            dma((8,)),
-            dma((NB - 1,)),
-            dma((NB - 1,)),
-            dma((ND - 1,)),
-            dma((ND - 1,)),
-            dma((ND - 1,)),
-            dma((ND - 1,)),
-            dma((ND - 1,)),
-            dma((ND - 1,)),
-            dma((NB - 1,)),
-            dma((NB - 1,)),
+            dma((3,)),
+            dma((3,)),
+            dma((4,)),
+            dma((4,)),
+            dma((NC - 1,)),
+            dma((NC - 1,)),
+            dma((NR - 1,)),
+            dma((NR - 1,)),
+            dma((NR - 1,)),
+            dma((NR - 1,)),
+            dma((NR - 1,)),
+            dma((NR - 1,)),
+            dma((NC - 1,)),
+            dma((NC - 1,)),
         ],
         compiler_params=pltpu.CompilerParams(
             collective_id=0, has_side_effects=True, vmem_limit_bytes=56 * 1024 * 1024

time: 61.7 us -> 60.2 us (0.976)
  the two profiles are of different devices: /device:TPU:1 before, /device:TPU:3 now
where the time goes in v3:
time: 60.2 us; the launch traced here: 60.1 us
  Pallas kernels  59.4 us (99%)
  between operations  0.64 us (1%)
    pallas_call x1, Pallas kernels, per_device(): pl.pallas_call(kernel, out_shape=shapes, in_specs=[hbm, hbm, hbm, hbm, hb...  55.4 us
    pallas_call x1, Pallas kernels, per_device(): pl.pallas_call(hand_over, out_shape=shapes, in_specs=[vmem, hbm, vmem, vm...  4.08 us

profile of v3, /device:TPU:3, one launch (start us, length us, event | category | flops | bytes accessed | tf_op | source)
XLA Modules:
  0.0 60.1 jit_solution(3728295205080676436)
XLA Ops:
  0.6 55.4 %shard_map.119 = (f32[1,16]{1,0:T(1,128)}, bf16[512,2048]{1,0:T(8,128)(2,1)}, f32[16,2048]{1,0:T(8,128)}, f32[16,128]{1,0:T(8,128)}, f32[16,1152]{1,0:T(8,128)}) custom-call(bf16[512,2048]{1,0:T(8,128)(2,1)} %tok_hbm.1, bf16[2048,2048]{1,0:T(8,128)(2,1)} %w_hbm.1, bf16[2048,1152]{1,0:T(8,128)(2,1)} %head_hbm.1, s32[1,512]{1,0:T(1,128)} %seg_hbm.1, ...), custom_call_target="tpu_custom_call" | custom-call | tf_op jit(solution)/shard_map/pallas_call | solution.py:534
  56.0 4.1 %shard_map.120 = (f32[1,16]{1,0:T(1,128)}, bf16[512,2048]{1,0:T(8,128)(2,1)}, f32[16,2048]{1,0:T(8,128)}, f32[16,128]{1,0:T(8,128)}, f32[16,1152]{1,0:T(8,128)}) custom-call(f32[1,16]{1,0:T(1,128)} %get-tuple-element.15.loss, bf16[512,2048]{1,0:T(8,128)(2,1)} %get-tuple-element.16.dtok, f32[16,2048]{1,0:T(8,128)} %get-tuple-element.17.dw, ...), custom_call_target="tpu_custom_call" | custom-call | tf_op jit(solution)/shard_map/pallas_call | solution.py:601

commit v4 on v3

--- a/solution.py
+++ b/solution.py
@@ -25,7 +25,7 @@
 PW = E + 128
 PARTS = 3
 ORDERS = (("x", "y", "z"), ("y", "z", "x"), ("z", "x", "y"))
-COLUMNS = ((0, 256), (256, 384), (640, 512))
+COLUMNS = ((0, 128), (128, 384), (512, 640))
 TN = 512
 UNROLL = True
 
@@ -242,10 +242,11 @@
 
     for i in range(DT // TN):
         if i == 2:
-            for p in range(PARTS):
+            for p in (2, 1, 0):
                 for k in range(3):
                     ring_wait(p, 0, k)
                 ring_send(p, 1)
+            for p in (2, 1, 0):
                 last_send(p, 0)
         wloads[i].wait()
         cols = pl.ds(i * TN, TN)
@@ -284,8 +285,8 @@
     cp = text_core(3, place)
     cp.start()
     sends.append(cp)
-    for k in (0, 2, 1):
-        for p in range(PARTS):
+    for p in (2, 1, 0):
+        for k in (0, 2, 1):
             ring_wait(p, 1, k)
             last_send(p, k + 1)
     for p in range(PARTS):
@@ -320,8 +321,8 @@
         cp = text_core(k, idx)
         cp.start()
         sends.append(cp)
-    for k in (0, 2, 1):
-        for p in range(PARTS):
+    for p in range(PARTS):
+        for k in (0, 2, 1):
             last_wait(p, k)
             core_send(p, k + 1)
     for p in range(PARTS):
@@ -500,20 +501,25 @@
         cp.wait_send()
 
 
-def hand_over(loss, dtok, dw, dgain, dimg, loss_out, dtok_out, dw_out, dgain_out, dimg_out, buf, ins, outs):
-    reads = []
-    for i in range(4):
-        cp = pltpu.make_async_copy(dtok.at[pl.ds(i * 128, 128), :], buf.at[pl.ds(i * 128, 128), :], ins.at[i])
+def hand_over(
+    loss, dtok, dw, dgain, dimg, loss_out, dtok_out, dw_out, dgain_out, dimg_out,
+    loss_buf, dtok_buf, dw_buf, dgain_buf, dimg_buf, ins, outs,
+):
+    trips = [
+        (dtok.at[rows, :], dtok_buf.at[rows, :], dtok_out.at[rows, :])
+        for rows in [pl.ds(i * 64, 64) for i in range(8)]
+    ]
+    trips += [
+        (dw, dw_buf, dw_out), (dimg, dimg_buf, dimg_out), (dgain, dgain_buf, dgain_out), (loss, loss_buf, loss_out)
+    ]
+    reads, writes = [], []
+    for i, (src, buf, _) in enumerate(trips):
+        cp = pltpu.make_async_copy(src, buf, ins.at[i])
         cp.start()
         reads.append(cp)
-    loss_out[...] = loss[...]
-    dw_out[...] = dw[...]
-    dgain_out[...] = dgain[...]
-    dimg_out[...] = dimg[...]
-    writes = []
-    for i in range(4):
+    for i, (_, buf, dst) in enumerate(trips):
         reads[i].wait()
-        cp = pltpu.make_async_copy(buf.at[pl.ds(i * 128, 128), :], dtok_out.at[pl.ds(i * 128, 128), :], outs.at[i])
+        cp = pltpu.make_async_copy(buf, dst, outs.at[i])
         cp.start()
         writes.append(cp)
     for cp in writes:
@@ -601,9 +607,9 @@
     loss, d_tokens, d_weight, d_gain, d_images = pl.pallas_call(
         hand_over,
         out_shape=shapes,
-        in_specs=[vmem, hbm, vmem, vmem, vmem],
-        out_specs=(vmem, hbm, vmem, vmem, vmem),
-        scratch_shapes=[pltpu.VMEM((ROWS, DT), bf16), dma((4,)), dma((4,))],
+        in_specs=[hbm] * 5,
+        out_specs=(hbm,) * 5,
+        scratch_shapes=[pltpu.VMEM(out.shape, out.dtype) for out in shapes] + [dma((12,)), dma((12,))],
         compiler_params=pltpu.CompilerParams(vmem_limit_bytes=56 * 1024 * 1024),
     )(*held)
     return loss.reshape(16), d_tokens, d_weight, d_gain.reshape(DT), d_images

time: 60.2 us -> 57.3 us (0.952)
  Pallas kernels: 59.4 us -> 56.5 us
    pallas_call x1, Pallas kernels: 4.08 us -> 2.53 us  [per_device(): pl.pallas_call(hand_over, out_shape=shapes, in_specs=[hbm] * 5, out_specs...]
    pallas_call x1, Pallas kernels: 55.4 us -> 54 us  [per_device(): pl.pallas_call(kernel, out_shape=shapes, in_specs=[hbm, hbm, hbm, hbm, hb...]
where the time goes in v4:
time: 57.3 us; the launch traced here: 57.2 us
  Pallas kernels  56.5 us (99%)
  between operations  0.64 us (1%)
    pallas_call x1, Pallas kernels, per_device(): pl.pallas_call(kernel, out_shape=shapes, in_specs=[hbm, hbm, hbm, hbm, hb...  54 us
    pallas_call x1, Pallas kernels, per_device(): pl.pallas_call(hand_over, out_shape=shapes, in_specs=[hbm] * 5, out_specs...  2.53 us

profile of v4, /device:TPU:3, one launch (start us, length us, event | category | flops | bytes accessed | tf_op | source)
XLA Modules:
  0.0 57.2 jit_solution(14288600585458420596)
XLA Ops:
  0.6 54.0 %shard_map.119 = (f32[1,16]{1,0:T(1,128)}, bf16[512,2048]{1,0:T(8,128)(2,1)}, f32[16,2048]{1,0:T(8,128)}, f32[16,128]{1,0:T(8,128)}, f32[16,1152]{1,0:T(8,128)}) custom-call(bf16[512,2048]{1,0:T(8,128)(2,1)} %tok_hbm.1, bf16[2048,2048]{1,0:T(8,128)(2,1)} %w_hbm.1, bf16[2048,1152]{1,0:T(8,128)(2,1)} %head_hbm.1, s32[1,512]{1,0:T(1,128)} %seg_hbm.1, ...), custom_call_target="tpu_custom_call" | custom-call | tf_op jit(solution)/shard_map/pallas_call | solution.py:540
  54.7 2.5 %shard_map.120 = (f32[1,16]{1,0:T(1,128)}, bf16[512,2048]{1,0:T(8,128)(2,1)}, f32[16,2048]{1,0:T(8,128)}, f32[16,128]{1,0:T(8,128)}, f32[16,1152]{1,0:T(8,128)}) custom-call(f32[1,16]{1,0:T(1,128)} %get-tuple-element.15.loss, bf16[512,2048]{1,0:T(8,128)(2,1)} %get-tuple-element.16.dtok, f32[16,2048]{1,0:T(8,128)} %get-tuple-element.17.dw, ...), custom_call_target="tpu_custom_call" | custom-call | tf_op jit(solution)/shard_map/pallas_call | solution.py:607

commit v5 on v4

--- a/solution.py
+++ b/solution.py
@@ -425,7 +425,17 @@
         stack[0:CAPS, rows] = dc
         return 0
 
-    lax.fori_loop(0, DT // TN, dcap_tile, 0)
+    lax.fori_loop(0, DT // TN, dcap_tile, 0, unroll=True)
+
+    def dnorm_tile(i, _):
+        rows = pl.ds(pl.multiple_of(i * TN, TN), TN)
+        hi, lo = split2(mm_nt(dcap[...], wv[rows, :]) * gain_ref[:, rows])
+        stack[CAPS : 2 * CAPS, rows] = hi
+        stack[2 * CAPS : 3 * CAPS, rows] = hi
+        stack[3 * CAPS : 4 * CAPS, rows] = lo
+        return 0
+
+    lax.fori_loop(0, DT // TN, dnorm_tile, 0, unroll=True)
 
     for k in range(NR - 1):
         row_wait(gbuf, k, g_send, g_recv)
@@ -436,16 +446,6 @@
         cp = column_copy(g2.at[place], g2.at[place], k, to, h_send, h_recv)
         cp.start()
         sends.append(cp)
-
-    def dnorm_tile(i, _):
-        rows = pl.ds(pl.multiple_of(i * TN, TN), TN)
-        hi, lo = split2(mm_nt(dcap[...], wv[rows, :]) * gain_ref[:, rows])
-        stack[CAPS : 2 * CAPS, rows] = hi
-        stack[2 * CAPS : 3 * CAPS, rows] = hi
-        stack[3 * CAPS : 4 * CAPS, rows] = lo
-        return 0
-
-    lax.fori_loop(0, DT // TN, dnorm_tile, 0)
 
     stores = []
     for i in range(4):
@@ -484,7 +484,7 @@
         dw_out[:, rows] = dw[0:16] + dw[16:32]
         return 0
 
-    lax.fori_loop(0, DT // TN, dw_tile, 0)
+    lax.fori_loop(0, DT // TN, dw_tile, 0, unroll=True)
 
     col = own_rows(jnp.where(xh == 0, gsum[0:1], gsum[1:2]) * (1.0 / TOTAL))
     loss_out[...] = jnp.sum(jnp.where(iota((16, 16), 0) == iota((16, 16), 1), col, 0.0), axis=0, keepdims=True)

time: 57.3 us -> 54.3 us (0.948)
  the two profiles are of different devices: /device:TPU:3 before, /device:TPU:1 now
where the time goes in v5:
time: 54.3 us; the launch traced here: 54.1 us
  Pallas kernels  53.5 us (99%)
  between operations  0.64 us (1%)
    pallas_call x1, Pallas kernels, per_device(): pl.pallas_call(kernel, out_shape=shapes, in_specs=[hbm, hbm, hbm, hbm, hb...  50.9 us
    pallas_call x1, Pallas kernels, per_device(): pl.pallas_call(hand_over, out_shape=shapes, in_specs=[hbm] * 5, out_specs...  2.53 us

profile of v5, /device:TPU:1, one launch (start us, length us, event | category | flops | bytes accessed | tf_op | source)
XLA Modules:
  0.0 54.1 jit_solution(12602781174059926795)
XLA Ops:
  0.6 50.9 %shard_map.119 = (f32[1,16]{1,0:T(1,128)}, bf16[512,2048]{1,0:T(8,128)(2,1)}, f32[16,2048]{1,0:T(8,128)}, f32[16,128]{1,0:T(8,128)}, f32[16,1152]{1,0:T(8,128)}) custom-call(bf16[512,2048]{1,0:T(8,128)(2,1)} %tok_hbm.1, bf16[2048,2048]{1,0:T(8,128)(2,1)} %w_hbm.1, bf16[2048,1152]{1,0:T(8,128)(2,1)} %head_hbm.1, s32[1,512]{1,0:T(1,128)} %seg_hbm.1, ...), custom_call_target="tpu_custom_call" | custom-call | tf_op jit(solution)/shard_map/pallas_call | solution.py:540
  51.6 2.5 %shard_map.120 = (f32[1,16]{1,0:T(1,128)}, bf16[512,2048]{1,0:T(8,128)(2,1)}, f32[16,2048]{1,0:T(8,128)}, f32[16,128]{1,0:T(8,128)}, f32[16,1152]{1,0:T(8,128)}) custom-call(f32[1,16]{1,0:T(1,128)} %get-tuple-element.15.loss, bf16[512,2048]{1,0:T(8,128)(2,1)} %get-tuple-element.16.dtok, f32[16,2048]{1,0:T(8,128)} %get-tuple-element.17.dw, ...), custom_call_target="tpu_custom_call" | custom-call | tf_op jit(solution)/shard_map/pallas_call | solution.py:607

commit v6 on v5

--- a/solution.py
+++ b/solution.py
@@ -49,10 +49,10 @@
 
 def kernel(
     tok_hbm, w_hbm, head_hbm, seg_hbm, own_hbm, img_hbm, gain_hbm, lp_ref,
-    loss_out, dtok_hbm, dw_out, dgain_out, dimg_out,
+    loss_out, dtok_hbm, dw_hbm, dgain_out, dimg_hbm,
     tok, wv, headv, img, lcol, segt, invc, xs, xp, npst, pooled, asrc, arcv, tbuf, dcap, stack,
-    seg_ref, own_ref, img_ref, gain_ref, stage, wh, coefs, zc, bacc, rsacc, c3as, c3ar, c3bs, c3br, gbuf, g2,
-    ld_sem, w_sem, in_sem, st_sem,
+    seg_ref, own_ref, img_ref, gain_ref, dw_buf, dimg_buf, stage, wh, coefs, zc, bacc, rsacc, c3as, c3ar, c3bs, c3br, gbuf, g2,
+    ld_sem, w_sem, in_sem, st_sem, out_sem,
     i_send, i_recv, j_send, j_recv, ic_send, ic_recv, t_send, t_recv, tc_send, tc_recv, a_send, a_recv,
     ca_send, ca_recv, cb_send, cb_recv, g_send, g_recv, h_send, h_recv,
 ):
@@ -466,7 +466,10 @@
     for k in range(NR - 1):
         row_wait(c3ar, k, ca_send, ca_recv)
     dimg = jnp.sum(c3ar[...].astype(f32), axis=0)
-    dimg_out[...] = img_inv * (dimg - img_unit * jnp.sum(img_unit * dimg, axis=1, keepdims=True))
+    dimg_buf[...] = img_inv * (dimg - img_unit * jnp.sum(img_unit * dimg, axis=1, keepdims=True))
+    cp = pltpu.make_async_copy(dimg_buf, dimg_hbm, out_sem.at[DT // TN])
+    cp.start()
+    stores.append(cp)
     for k in range(NR - 1):
         row_wait(c3br, k, cb_send, cb_recv)
     mine = iota((16, 128), 1) == iota((16, 128), 0) + 16 * d
@@ -478,13 +481,13 @@
     hi, lo = split2(jnp.sum(c3br[...].astype(f32), axis=0) * gain_col)
     both = jnp.concatenate([hi, lo], axis=0)
 
-    def dw_tile(i, _):
-        rows = pl.ds(pl.multiple_of(i * TN, TN), TN)
+    for i in range(DT // TN):
+        rows = pl.ds(i * TN, TN)
         dw = mm_nt(both, headv[rows, :])
-        dw_out[:, rows] = dw[0:16] + dw[16:32]
-        return 0
-
-    lax.fori_loop(0, DT // TN, dw_tile, 0, unroll=True)
+        dw_buf[:, rows] = dw[0:16] + dw[16:32]
+        cp = pltpu.make_async_copy(dw_buf.at[:, rows], dw_hbm.at[:, rows], out_sem.at[i])
+        cp.start()
+        stores.append(cp)
 
     col = own_rows(jnp.where(xh == 0, gsum[0:1], gsum[1:2]) * (1.0 / TOTAL))
     loss_out[...] = jnp.sum(jnp.where(iota((16, 16), 0) == iota((16, 16), 1), col, 0.0), axis=0, keepdims=True)
@@ -541,7 +544,7 @@
         kernel,
         out_shape=shapes,
         in_specs=[hbm, hbm, hbm, hbm, hbm, hbm, hbm, pl.BlockSpec(memory_space=pltpu.SMEM)],
-        out_specs=(vmem, hbm, vmem, vmem, vmem),
+        out_specs=(vmem, hbm, hbm, vmem, hbm),
         scratch_shapes=[
             pltpu.VMEM((ROWS, DT), bf16),
             pltpu.VMEM((DT, DT), bf16),
@@ -563,6 +566,8 @@
             pltpu.VMEM((1, CAPS), jnp.int32),
             pltpu.VMEM((16, E), bf16),
             pltpu.VMEM((1, DT), f32),
+            pltpu.VMEM((16, DT), f32),
+            pltpu.VMEM((16, E), f32),
             pltpu.VMEM((ROWS, DT), bf16),
             pltpu.VMEM((GR, E), f32),
             pltpu.VMEM((SLOTS, 512), bf16),
@@ -579,6 +584,7 @@
             dma((DT // TN,)),
             dma((4,)),
             dma((4,)),
+            dma((DT // TN + 1,)),
             dma((PARTS, 2, 3)),
             dma((PARTS, 2, 3)),
             dma((PARTS, 4, 3)),

time: 54.3 us -> 54.8 us (level)
  no operation moved by 1% of the time
where the time goes in v6:
time: 54.8 us; the launch traced here: 54.6 us
  Pallas kernels  54 us (99%)
  between operations  0.64 us (1%)
    pallas_call x1, Pallas kernels, per_device(): pl.pallas_call(kernel, out_shape=shapes, in_specs=[hbm, hbm, hbm, hbm, hb...  51.5 us
    pallas_call x1, Pallas kernels, per_device(): pl.pallas_call(hand_over, out_shape=shapes, in_specs=[hbm] * 5, out_specs...  2.53 us

profile of v6, /device:TPU:1, one launch (start us, length us, event | category | flops | bytes accessed | tf_op | source)
XLA Modules:
  0.0 54.6 jit_solution(6053105106652616060)
XLA Ops:
  0.6 51.5 %shard_map.119 = (f32[1,16]{1,0:T(1,128)}, bf16[512,2048]{1,0:T(8,128)(2,1)}, f32[16,2048]{1,0:T(8,128)}, f32[16,128]{1,0:T(8,128)}, f32[16,1152]{1,0:T(8,128)}) custom-call(bf16[512,2048]{1,0:T(8,128)(2,1)} %tok_hbm.1, bf16[2048,2048]{1,0:T(8,128)(2,1)} %w_hbm.1, bf16[2048,1152]{1,0:T(8,128)(2,1)} %head_hbm.1, s32[1,512]{1,0:T(1,128)} %seg_hbm.1, ...), custom_call_target="tpu_custom_call" | custom-call | tf_op jit(solution)/shard_map/pallas_call | solution.py:543
  52.1 2.5 %shard_map.120 = (f32[1,16]{1,0:T(1,128)}, bf16[512,2048]{1,0:T(8,128)(2,1)}, f32[16,2048]{1,0:T(8,128)}, f32[16,128]{1,0:T(8,128)}, f32[16,1152]{1,0:T(8,128)}) custom-call(f32[1,16]{1,0:T(1,128)} %get-tuple-element.15.loss, bf16[512,2048]{1,0:T(8,128)(2,1)} %get-tuple-element.16.dtok, f32[16,2048]{1,0:T(8,128)} %get-tuple-element.17.dw, ...), custom_call_target="tpu_custom_call" | custom-call | tf_op jit(solution)/shard_map/pallas_call | solution.py:613
